TPU v7x, 128 devices: a whole 4x4x4 slice. The times are simulated.
128 devices in a mesh: grp: 2 (over core), dev: 64 (over z, x, y).
Axes of the slice: x: 4, y: 4, z: 4, core: 2. Of those that a mesh axis runs over, the one named last changes fastest.
Arguments:
- queries: bfloat16 [2048, 8192], P(('grp', 'dev')), may hold values from -27 to 27
- cache_keys: bfloat16 [2048, 32, 512], P(('grp', 'dev')), may hold values from -6 to 6
- cache_values: bfloat16 [2048, 32, 512], P(('grp', 'dev')), may hold values from -6 to 6
- own_len: int32 [2048], P(('grp', 'dev')), may hold values from 2 to 32, as said below
- ext_keys: bfloat16 [2048, 32, 512], P(('grp', 'dev')), may hold values from -6 to 6
- ext_values: bfloat16 [2048, 32, 512], P(('grp', 'dev')), may hold values from -6 to 6
- ext_len: int32 [2048], P(('grp', 'dev')), may hold values from 0 to 32, as said below
- new_key: bfloat16 [2048, 512], P(('grp', 'dev')), may hold values from -6 to 6
- new_value: bfloat16 [2048, 512], P(('grp', 'dev')), may hold values from -6 to 6
- moe_input: bfloat16 [2048, 4096], P(('grp', 'dev')), may hold values from -6 to 6
- expert_ids: int32 [2048, 8], P(('grp', 'dev')), may hold values from 0 to 127, all different within a row; in each aligned block of 16 rows (0 to 15, 16 to 31, ...) at most 2 rows name the same one
- route_scores: float32 [2048, 8], P(('grp', 'dev')), may hold values from 0.05 to 1
- w_gate: bfloat16 [128, 4096, 768], P(('grp', 'dev')), may hold values from -0.09375 to 0.09375
- w_up: bfloat16 [128, 4096, 768], P(('grp', 'dev')), may hold values from -0.09375 to 0.09375
- w_down: bfloat16 [128, 768, 4096], P(('grp', 'dev')), may hold values from -0.21875 to 0.21875
Outputs:
- attention_out: bfloat16 [2048, 8192], P(('grp', 'dev'))
- moe_out: bfloat16 [2048, 4096], P(('grp', 'dev'))
Inputs may be any that keep to these rules, and one draw needn't show every extreme that they name: own_len[r] is 32 wherever ext_len[p(r)] is positive; some row of every device has 32. ext_len at a position is zero where the paired row has no continuation; the first position of every device has 32. `expert_ids`: each row names 8 different experts; among the rows of one device no expert is named more than 2 times, a bound that some block reaches.
All inputs are finite; a program needn't handle non-finite values.
Results may differ from a plain program's by a relative error of at most 0.008.
Values may be sent and summed in bfloat16 or wider, within the bound.
No kernel may reach another device: no remote copies, remote signals or barrier semaphores. Data moves between devices by JAX's collectives and lax.ppermute only.
A program may use at most 128 MiB of HBM per device.

v0:
```python
import jax
import jax.numpy as jnp
from jax import lax
from jax.sharding import PartitionSpec as P

QH = 64
KVH = 4
HD = 128


def partner(block, axis, apart):
    count = lax.axis_size(axis)
    route = []
    for low in range(count):
        high = low | 1 << apart
        if high != low and high < count:
            route += [(low, high), (high, low)]
    return lax.ppermute(block, axis, route)


def partial_softmax(queries, keys, values, live_slots):
    row_count = queries.shape[0]
    groups = QH // KVH
    query_flat = queries.astype(jnp.float32).reshape(row_count, KVH, groups, HD)
    key_flat = keys.astype(jnp.float32).reshape(row_count, keys.shape[1], KVH, HD)
    value_flat = values.astype(jnp.float32).reshape(row_count, values.shape[1], KVH, HD)
    scores = jnp.einsum("rkgh,rskh->rkgs", query_flat, key_flat) / jnp.sqrt(jnp.float32(HD))
    live_mask = live_slots[:, None, None, :]
    row_max = jnp.max(jnp.where(live_mask, scores, -jnp.inf), axis=-1)
    row_max = jnp.where(jnp.isfinite(row_max), row_max, -1e30)
    weights = jnp.where(live_mask, jnp.exp(scores - row_max[..., None]), 0.0)
    row_total = jnp.sum(weights, axis=-1)
    numerator = jnp.einsum("rkgs,rskh->rkgh", weights, value_flat)
    return (
        row_max.reshape(row_count, QH),
        row_total.reshape(row_count, QH),
        numerator.reshape(row_count, QH, HD),
    )


def merge_parts(first, second):
    max_one, total_one, numer_one = first
    max_two, total_two, numer_two = second
    largest = jnp.maximum(max_one, max_two)
    scale_one = jnp.exp(max_one - largest)
    scale_two = jnp.exp(max_two - largest)
    row_total = total_one * scale_one + total_two * scale_two
    numerator = numer_one * scale_one[..., None] + numer_two * scale_two[..., None]
    merged = numerator / row_total[..., None]
    return merged.reshape(merged.shape[0], -1).astype(jnp.bfloat16)


def body(
    queries,
    cache_keys,
    cache_values,
    own_len,
    ext_keys,
    ext_values,
    ext_len,
    new_key,
    new_value,
    moe_input,
    expert_ids,
    route_scores,
    w_gate,
    w_up,
    w_down,
):
    slot_count = cache_keys.shape[1]
    positions = jnp.arange(slot_count + 1, dtype=jnp.int32)[None, :]
    own_live = (positions < own_len[:, None]) | (positions == slot_count)
    own_keys = jnp.concatenate([cache_keys, new_key[:, None, :]], axis=1)
    own_values = jnp.concatenate([cache_values, new_value[:, None, :]], axis=1)
    own_part = partial_softmax(queries, own_keys, own_values, own_live)
    far_positions = positions[:, :slot_count]
    far_keys, far_values, far_len = partner((ext_keys, ext_values, ext_len), "dev", 0)
    far_part = partial_softmax(queries, far_keys, far_values, far_positions < far_len[:, None])
    attention_out = merge_parts(own_part, far_part)
    devices = lax.axis_size("grp") * lax.axis_size("dev")
    local_experts = w_gate.shape[0]
    experts = devices * local_experts
    row_count, top_count = expert_ids.shape
    capacity = max(2, 2 * row_count * top_count // experts)
    flat_ids = expert_ids.reshape(-1)
    onehot = (flat_ids[:, None] == jnp.arange(experts, dtype=jnp.int32)[None, :]).astype(jnp.int32)
    slot_rank = jnp.sum(jnp.cumsum(onehot, axis=0) * onehot, axis=1) - 1
    slot_of = flat_ids * capacity + slot_rank
    assign_rows = jnp.arange(row_count * top_count, dtype=jnp.int32) // top_count
    sources = jnp.full((experts * capacity,), row_count, jnp.int32).at[slot_of].set(assign_rows)
    padded = jnp.concatenate(
        [moe_input, jnp.zeros((1, moe_input.shape[1]), moe_input.dtype)], axis=0
    )
    outgoing = padded[sources].reshape(devices, local_experts, capacity, -1)
    arrived = lax.all_to_all(outgoing, ("grp", "dev"), split_axis=0, concat_axis=0, tiled=True)
    gate_act = jnp.einsum("necd,edf->necf", arrived, w_gate, preferred_element_type=jnp.float32)
    up_act = jnp.einsum("necd,edf->necf", arrived, w_up, preferred_element_type=jnp.float32)
    hidden = (jax.nn.silu(gate_act) * up_act).astype(jnp.bfloat16)
    returned = lax.all_to_all(
        jnp.einsum("necf,efd->necd", hidden, w_down, preferred_element_type=jnp.float32).astype(
            jnp.bfloat16
        ),
        ("grp", "dev"),
        split_axis=0,
        concat_axis=0,
        tiled=True,
    )
    picked = returned.reshape(experts * capacity, -1)[slot_of].reshape(row_count, top_count, -1)
    route_weights = route_scores / jnp.sum(route_scores, axis=1, keepdims=True)
    moe_out = jnp.sum(route_weights[:, :, None] * picked.astype(jnp.float32), axis=1).astype(
        jnp.bfloat16
    )
    return (attention_out, moe_out)


def solution(mesh):
    placed = (
        P(("grp", "dev"), None),
        P(("grp", "dev"), None, None),
        P(("grp", "dev"), None, None),
        P(("grp", "dev")),
        P(("grp", "dev"), None, None),
        P(("grp", "dev"), None, None),
        P(("grp", "dev")),
        P(("grp", "dev"), None),
        P(("grp", "dev"), None),
        P(("grp", "dev"), None),
        P(("grp", "dev"), None),
        P(("grp", "dev"), None),
        P(("grp", "dev"), None, None),
        P(("grp", "dev"), None, None),
        P(("grp", "dev"), None, None),
    )
    return jax.shard_map(
        body,
        mesh=mesh,
        in_specs=placed,
        out_specs=(P(("grp", "dev"), None), P(("grp", "dev"), None)),
        check_vma=False,
    )
```

profile of v0, /device:TPU:5, one launch (start us, length us, event | category | flops | bytes accessed | tf_op | source)
XLA Modules:
  0.0 122.1 jit_solution(1688402841184738736)
XLA Ops:
  0.6 0.0 copy-start
  0.6 1.4 %collective-permute-start = (s32[16]{0:T(128)}, s32[16]{0:T(128)S(1)}, u32[]{:S(2)}, u32[]{:S(2)}) collective-permute-start(s32[16]{0:T(128)} %param.21), channel_id=1, source_target_pairs={{0,1},{1,0},{2,3},{3,2},{4,5},{5,4},{6,7},{7,6},{8,9},{9,8},{10,11... | collective-permute-start | bytes 200 | tf_op jit(solution)/shard_map/ppermute | solution.py:18
  2.0 0.2 collective-permute-start.1
  2.2 1.3 %collective-permute-start.2 = (bf16[16,32,512]{2,1,0:T(8,128)(2,1)}, bf16[16,32,512]{2,1,0:T(8,128)(2,1)}, u32[]{:S(2)}, u32[]{:S(2)}) collective-permute-start(bf16[16,32,512]{2,1,0:T(8,128)(2,1)} %param.20), channel_id=1, source_target_pairs={{0,1},{1,0},{2,3},{3,2},{4,5},{5,4},{6,7},{7,6},{8,9},{9,8},{10,11... | collective-permute-start | bytes 1572872 | tf_op jit(solution)/shard_map/ppermute | solution.py:18
  3.5 0.8 copy.39
  4.2 0.7 broadcast_multiply_fusion
  4.9 0.1 eq.28
  5.0 0.1 fusion.72
  5.1 0.2 reduce_window_sum.11
  5.3 0.2 select_reduce_fusion.2
  5.5 0.1 copy.38
  5.5 0.1 mul.81
  5.7 1.0 scatter_custom_fusion
  6.7 0.9 concatenate.25
  7.6 1.8 %gather_fusion = bf16[256,4096]{1,0:T(8,128)(2,1)S(1)} fusion(bf16[17,4096]{1,0:T(8,128)(2,1)S(1)} %concatenate.25, s32[1024]{0:T(1024)S(1)} %pad_clamp_fusion.1), kind=kCustom, calls=%fused_computation | custom fusion | bytes 4195328 | tf_op jit(solution)/shard_map/gather | solution.py:94
  9.4 2.7 %reshape.237 = bf16[128,1,2,4096]{3,2,0,1:T(2,128)(2,1)} reshape(bf16[256,4096]{1,0:T(8,128)(2,1)S(1)} %gather_fusion) | data formatting | bytes 4194304 | tf_op jit(solution)/shard_map/reshape | solution.py:94
  12.1 0.0 copy-start.3
  12.1 0.0 copy-start.4
  12.1 0.0 copy-start.7
  12.1 11.5 %all-to-all-start = ((bf16[128,1,2,4096]{3,2,1,0:T(2,128)(2,1)}), bf16[128,1,2,4096]{3,2,1,0:T(2,128)(2,1)S(1)}, u32[]{:S(2)}, u32[]{:S(2)}) async-start(bf16[128,1,2,4096]{3,2,1,0:T(2,128)(2,1)} %bitcast.143), calls=%async_computation | async-start | bytes 4194304 | tf_op jit(solution)/shard_map/all_to_all | solution.py:95
  23.7 0.0 copy-start.6
  23.7 0.0 copy-done.3
  23.7 0.0 copy-done
  23.8 0.9 copy_bitcast_fusion.1
  24.6 0.0 copy-done.4
  24.6 0.0 copy-start.5
  24.7 0.0 copy-done.7
  24.7 0.1 fusion.75
  24.8 1.6 %select_reduce_fusion.1 = (f32[16,4,16]{2,1,0:T(4,128)S(1)}, f32[16,4,33,16]{2,3,1,0:T(8,128)S(1)}) fusion(pred[16,33]{1,0:T(8,128)(4,1)S(1)} %fusion.75, bf16[16,4,16,128]{3,2,1,0:T(8,128)(2,1)S(1)} %bitcast.148, bf16[16,1,4,128]{3,1,2,0:T(2,128)(2,1)S(1)} %concatenate.26, bf16[16,32,4,128]{3,1,2,0:T(8,128)(2,1)} %copy_bitcast_fusion.1), kind=kOutput, calls=%fused_computation.49 | convolution fusion | flops 9832448 | bytes 942608 | tf_op jit(solution)/shard_map/rkgh,rskh->rkgs/dot_general | solution.py:27
  26.4 0.0 copy-done.6
  26.4 0.4 fusion.63
  26.9 1.9 %copy_bitcast_fusion = bf16[16,32,4,128]{3,1,2,0:T(8,128)(2,1)} fusion(bf16[16,32,512]{2,1,0:T(8,128)(2,1)} %param.17), kind=kLoop, calls=%fused_computation.44 | loop fusion | bytes 1048576 | tf_op jit(solution)/shard_map/concatenate | solution.py:74
  28.8 0.1 reduce_max.23
  28.9 0.1 reshape.235
  29.0 0.0 copy-done.5
  29.0 2.2 %fusion.52 = f32[16,4,16,128]{3,2,1,0:T(8,128)} fusion(bf16[16,1,4,128]{3,1,2,0:T(2,128)(2,1)S(1)} %concatenate.27, bf16[16,32,4,128]{3,1,2,0:T(8,128)(2,1)} %copy_bitcast_fusion, f32[16,4,33,16]{2,3,1,0:T(8,128)S(1)} %get-tuple-element.8, f32[16,4,16]{2,1,0:T(4,128)S(1)} %is-finite_select_fusion.1, pred[16,33]{1,0:T(8,128)(4,1)S(1)} %fusion.75), kind=kOutput, calls=%fused_computation.30 | convolution fusion | flops 9799680 | bytes 1204752 | tf_op jit(solution)/shard_map/rkgs,rskh->rkgh/dot_general | solution.py:33
  31.2 0.1 copy.37
  31.3 0.0 collective-permute-done
  31.3 0.1 broadcast_compare_fusion
  31.4 0.0 collective-permute-done.1
  31.4 1.5 %select_reduce_fusion = (f32[16,4,16]{2,1,0:T(4,128)S(1)}, f32[16,4,16,32]{3,2,1,0:T(8,128)S(1)}) fusion(pred[16,32]{1,0:T(8,128)(4,1)S(1)} %broadcast_compare_fusion, bf16[16,4,16,128]{3,2,1,0:T(8,128)(2,1)S(1)} %bitcast.149, bf16[16,32,512]{2,1,0:T(8,128)(2,1)} %collective-permute-done.1), kind=kOutput, calls=%fused_computation.47 | convolution fusion | flops 8485888 | bytes 922112 | tf_op jit(solution)/shard_map/rkgh,rskh->rkgs/dot_general | solution.py:27
  32.9 0.1 reduce_max.25
  33.0 0.4 fusion.64
  33.4 0.1 reshape.236
  33.5 0.0 collective-permute-done.2
  33.5 2.2 %fusion.58 = f32[16,4,16,128]{3,2,1,0:T(8,128)} fusion(f32[16,4,16,32]{3,2,1,0:T(8,128)S(1)} %get-tuple-element.6, f32[16,4,16]{2,1,0:T(4,128)S(1)} %is-finite_select_fusion, pred[16,32]{1,0:T(8,128)(4,1)S(1)} %broadcast_compare_fusion, bf16[16,32,512]{2,1,0:T(8,128)(2,1)} %collective-permute-done.2), kind=kOutput, calls=%fused_computation.39 | convolution fusion | flops 8454144 | bytes 1184256 | tf_op jit(solution)/shard_map/rkgs,rskh->rkgh/dot_general | solution.py:33
  35.7 19.1 %all-to-all-done = bf16[128,1,2,4096]{3,2,1,0:T(2,128)(2,1)S(1)} async-done(((bf16[128,1,2,4096]{3,2,1,0:T(2,128)(2,1)}), bf16[128,1,2,4096]{3,2,1,0:T(2,128)(2,1)S(1)}, u32[]{:S(2)}, u32[]{:S(2)}) %all-to-all-start) | async-done | bytes 2097184 | tf_op jit(solution)/shard_map/all_to_all | solution.py:95
  54.8 6.4 %fusion.17 = f32[128,1,2,768]{3,0,2,1:T(8,128)S(1)} fusion(bf16[1,4096,768]{2,1,0:T(8,128)(2,1)} %param.27, bf16[128,1,2,4096]{3,2,1,0:T(2,128)(2,1)S(1)} %all-to-all-done), kind=kOutput, calls=%fused_computation.17 | convolution fusion | flops 1610612736 | bytes 9175040 | tf_op jit(solution)/shard_map/necd,edf->necf/dot_general | solution.py:96
  61.2 12.0 %fusion.9 = bf16[128,1,2,4096]{3,0,2,1:T(8,128)(2,1)} fusion(bf16[1,768,4096]{2,1,0:T(8,128)(2,1)} %param.29, bf16[1,4096,768]{2,1,0:T(8,128)(2,1)} %param.28, bf16[128,1,2,4096]{3,2,1,0:T(2,128)(2,1)S(1)} %all-to-all-done, f32[128,1,2,768]{3,0,2,1:T(8,128)S(1)} %fusion.17), kind=kOutput, calls=%fused_computation.10 | convolution fusion | flops 3223453696 | bytes 17563648 | tf_op jit(solution)/shard_map/necf,efd->necd/dot_general | solution.py:100
  73.2 5.4 %copy.42 = bf16[128,1,2,4096]{3,2,1,0:T(2,128)(2,1)} copy(bf16[128,1,2,4096]{3,0,2,1:T(8,128)(2,1)} %fusion.9) | data formatting | bytes 4194304 | tf_op jit(solution)/shard_map/convert_element_type | solution.py:100
  78.6 0.0 copy-start.1
  78.6 0.0 copy-start.2
  78.6 6.9 %all-to-all-start.1 = ((bf16[128,1,2,4096]{3,2,1,0:T(2,128)(2,1)}), bf16[128,1,2,4096]{3,2,1,0:T(2,128)(2,1)}, u32[]{:S(2)}, u32[]{:S(2)}) async-start(bf16[128,1,2,4096]{3,2,1,0:T(2,128)(2,1)} %copy.42), calls=%async_computation.1 | async-start | bytes 4194304 | tf_op jit(solution)/shard_map/all_to_all | solution.py:99
  85.6 0.2 mul.70
  85.8 0.2 mul.73
  86.0 0.2 div.47
  86.2 0.0 copy-done.1
  86.2 0.0 copy-done.2
  86.2 2.1 %fusion.56 = bf16[16,8192]{1,0:T(8,128)(2,1)} fusion(f32[2,8,64,128]{3,2,1,0:T(8,128)S(1)} %bitcast.147, f32[2,8,64,128]{3,2,1,0:T(8,128)S(1)} %bitcast.146, f32[2,8,64,128]{3,2,1,0:T(8,128)S(1)} %bitcast.144, f32[2,8,64,128]{3,2,1,0:T(8,128)S(1)} %bitcast.145, f32[2,8,64,128]{3,2,1,0:T(8,128)S(1)} %bitcast.150), kind=kLoop, calls=%fused_computation.35 | loop fusion | flops 655360 | bytes 2883584 | tf_op jit(solution)/shard_map/convert_element_type | solution.py:50
  88.3 26.2 %all-to-all-done.1 = bf16[128,1,2,4096]{3,2,1,0:T(2,128)(2,1)} async-done(((bf16[128,1,2,4096]{3,2,1,0:T(2,128)(2,1)}), bf16[128,1,2,4096]{3,2,1,0:T(2,128)(2,1)}, u32[]{:S(2)}, u32[]{:S(2)}) %all-to-all-start.1) | async-done | bytes 2097184 | tf_op jit(solution)/shard_map/all_to_all | solution.py:99
  114.5 2.7 %reshape.243 = bf16[256,4096]{1,0:T(8,128)(2,1)S(1)} reshape(bf16[128,1,2,4096]{3,2,1,0:T(2,128)(2,1)} %all-to-all-done.1) | data formatting | bytes 4194304 | tf_op jit(solution)/shard_map/reshape | solution.py:108
  117.2 2.2 %gather_fusion.1 = bf16[128,4096]{1,0:T(8,128)(2,1)} fusion(bf16[256,4096]{1,0:T(8,128)(2,1)S(1)} %reshape.243, s32[1024]{0:T(1024)S(1)} %pad_clamp_fusion), kind=kCustom, calls=%fused_computation.1 | custom fusion | bytes 2097664 | tf_op jit(solution)/shard_map/gather | solution.py:108
  119.4 2.7 %fusion.12 = bf16[16,4096]{1,0:T(8,128)(2,1)} fusion(bf16[128,4096]{1,0:T(8,128)(2,1)} %gather_fusion.1, f32[16,8]{1,0:T(8,128)S(1)} %copy.37), kind=kLoop, calls=%fused_computation.12 | loop fusion | flops 1507328 | bytes 1180160 | tf_op jit(solution)/shard_map/reduce_sum | solution.py:110
  (16 shorter events, 0.2 us)
Async XLA Ops:
  0.6 23.1 %copy-start = (bf16[16,32,512]{2,1,0:T(8,128)(2,1)S(1)}, bf16[16,32,512]{2,1,0:T(8,128)(2,1)}, u32[]{:S(2)}) copy-start(bf16[16,32,512]{2,1,0:T(8,128)(2,1)} %param.16) | copy-start | bytes 1572868
  0.6 30.6 %collective-permute-start = (s32[16]{0:T(128)}, s32[16]{0:T(128)S(1)}, u32[]{:S(2)}, u32[]{:S(2)}) collective-permute-start(s32[16]{0:T(128)} %param.21), channel_id=1, source_target_pairs={{0,1},{1,0},{2,3},{3,2},{4,5},{5,4},{6,7},{7,6},{8,9},{9,8},{10,11... | collective-permute-start | bytes 200 | tf_op jit(solution)/shard_map/ppermute | solution.py:18
  2.0 29.4 %collective-permute-start.1 = (bf16[16,32,512]{2,1,0:T(8,128)(2,1)}, bf16[16,32,512]{2,1,0:T(8,128)(2,1)}, u32[]{:S(2)}, u32[]{:S(2)}) collective-permute-start(bf16[16,32,512]{2,1,0:T(8,128)(2,1)} %param.19), channel_id=1, source_target_pairs={{0,1},{1,0},{2,3},{3,2},{4,5},{5,4},{6,7},{7,6},{8,9},{9,8},{10,11... | collective-permute-start | bytes 1572872 | tf_op jit(solution)/shard_map/ppermute | solution.py:18
  2.2 31.3 %collective-permute-start.2 = (bf16[16,32,512]{2,1,0:T(8,128)(2,1)}, bf16[16,32,512]{2,1,0:T(8,128)(2,1)}, u32[]{:S(2)}, u32[]{:S(2)}) collective-permute-start(bf16[16,32,512]{2,1,0:T(8,128)(2,1)} %param.20), channel_id=1, source_target_pairs={{0,1},{1,0},{2,3},{3,2},{4,5},{5,4},{6,7},{7,6},{8,9},{9,8},{10,11... | collective-permute-start | bytes 1572872 | tf_op jit(solution)/shard_map/ppermute | solution.py:18
  12.1 11.6 %copy-start.3 = (bf16[16,8192]{1,0:T(8,128)(2,1)S(1)}, bf16[16,8192]{1,0:T(8,128)(2,1)}, u32[]{:S(2)}) copy-start(bf16[16,8192]{1,0:T(8,128)(2,1)} %param.15) | copy-start | bytes 786436
  12.1 12.5 %copy-start.4 = (bf16[16,512]{1,0:T(8,128)(2,1)S(1)}, bf16[16,512]{1,0:T(8,128)(2,1)}, u32[]{:S(2)}) copy-start(bf16[16,512]{1,0:T(8,128)(2,1)} %param.22) | copy-start | bytes 49156
  12.1 12.6 %copy-start.7 = (s32[16]{0:T(128)S(1)}, s32[16]{0:T(128)}, u32[]{:S(2)}) copy-start(s32[16]{0:T(128)} %param.18) | copy-start | bytes 196
  12.1 42.7 %all-to-all-start = ((bf16[128,1,2,4096]{3,2,1,0:T(2,128)(2,1)}), bf16[128,1,2,4096]{3,2,1,0:T(2,128)(2,1)S(1)}, u32[]{:S(2)}, u32[]{:S(2)}) async-start(bf16[128,1,2,4096]{3,2,1,0:T(2,128)(2,1)} %bitcast.143), calls=%async_computation | async-start | bytes 4194304 | tf_op jit(solution)/shard_map/all_to_all | solution.py:95
  23.7 2.7 %copy-start.6 = (f32[16,8]{0,1:T(8,128)S(1)}, f32[16,8]{0,1:T(8,128)}, u32[]{:S(2)}) copy-start(f32[16,8]{0,1:T(8,128)} %param.26) | copy-start | bytes 1540
  24.6 4.3 %copy-start.5 = (bf16[16,512]{1,0:T(8,128)(2,1)S(1)}, bf16[16,512]{1,0:T(8,128)(2,1)}, u32[]{:S(2)}) copy-start(bf16[16,512]{1,0:T(8,128)(2,1)} %param.23) | copy-start | bytes 49156
  78.6 7.6 %copy-start.1 = (f32[16,4,16,128]{3,2,1,0:T(8,128)S(1)}, f32[16,4,16,128]{3,2,1,0:T(8,128)}, u32[]{:S(2)}) copy-start(f32[16,4,16,128]{3,2,1,0:T(8,128)} %fusion.58) | copy-start | bytes 1572868
  78.6 7.6 %copy-start.2 = (f32[16,4,16,128]{3,2,1,0:T(8,128)S(1)}, f32[16,4,16,128]{3,2,1,0:T(8,128)}, u32[]{:S(2)}) copy-start(f32[16,4,16,128]{3,2,1,0:T(8,128)} %fusion.52) | copy-start | bytes 1572868
  78.6 35.9 %all-to-all-start.1 = ((bf16[128,1,2,4096]{3,2,1,0:T(2,128)(2,1)}), bf16[128,1,2,4096]{3,2,1,0:T(2,128)(2,1)}, u32[]{:S(2)}, u32[]{:S(2)}) async-start(bf16[128,1,2,4096]{3,2,1,0:T(2,128)(2,1)} %copy.42), calls=%async_computation.1 | async-start | bytes 4194304 | tf_op jit(solution)/shard_map/all_to_all | solution.py:99
where the time goes:
time: 123 us; the launch traced here: 122 us
  waiting for transfers between devices  45.3 us (37%)
  matrix products  26 us (21%)
  local copies, waits for them, and re-layouts  21.6 us (18%)
  starting transfers between devices  21.3 us (17%)
  other arithmetic  6.97 us (6%)
    all_to_all x1, waiting for transfers between devices, body(): lax.all_to_all(jnp.einsum('necf,efd->necd', hidden, w_down, preferred_ele...  26.2 us
    all_to_all x1, waiting for transfers between devices, body(): lax.all_to_all(outgoing, ('grp', 'dev'), split_axis=0, concat_axis=0, til...  19.1 us
    dot_general x1, matrix products, body(): jnp.einsum('necf,efd->necd', hidden, w_down, preferred_element_type=jnp.f...  12 us
    all_to_all x1, starting transfers between devices, body(): lax.all_to_all(outgoing, ('grp', 'dev'), split_axis=0, concat_axis=0, til...  11.5 us
    all_to_all x1, starting transfers between devices, body(): lax.all_to_all(jnp.einsum('necf,efd->necd', hidden, w_down, preferred_ele...  6.93 us
    dot_general x1, matrix products, body(): jnp.einsum('necd,edf->necf', arrived, w_gate, preferred_element_type=jnp....  6.39 us
    convert_element_type x1, local copies, waits for them, and re-layouts, body(): jnp.einsum('necf,efd->necd', hidden, w_down, preferred_element_type=jnp.f...  5.35 us
    dot_general x2, matrix products, partial_softmax(): numerator = jnp.einsum('rkgs,rskh->rkgh', weights, value_flat)  4.47 us
  transfers between devices with their start and end apart: 5, of which 2 were waited for; matrix products, arithmetic and copies ran while one was open for 19% of the time, Pallas kernels for 0%

commit v1 on v0

--- a/solution.py
+++ b/solution.py
@@ -1,11 +1,23 @@
 import jax
 import jax.numpy as jnp
 from jax import lax
+from jax.experimental import pallas as pl
+from jax.experimental.pallas import tpu as pltpu
 from jax.sharding import PartitionSpec as P
 
 QH = 64
 KVH = 4
 HD = 128
+DMODEL = 4096
+FF = 768
+TOPK = 8
+EXPERTS = 128
+ROW_BLOCK = 16
+LANES = 128
+GROUPS = 4
+CHUNK = 64
+PREP_PIECES = 4
+COMBINE_STEPS = 4
 
 
 def partner(block, axis, apart):
@@ -48,6 +60,291 @@
     numerator = numer_one * scale_one[..., None] + numer_two * scale_two[..., None]
     merged = numerator / row_total[..., None]
     return merged.reshape(merged.shape[0], -1).astype(jnp.bfloat16)
+
+
+def slot_index_kernel(ids_ref, x_ref, out_ref, stack_ref, first_ref, second_ref, sem):
+    lane = lax.broadcasted_iota(jnp.int32, (ROW_BLOCK, LANES), 1)
+    row = lax.broadcasted_iota(jnp.int32, (ROW_BLOCK, LANES), 0)
+    spread = (lane % ROW_BLOCK == row).astype(jnp.bfloat16)
+    ids = ids_ref[...].astype(jnp.float32).astype(jnp.bfloat16)
+    named = lax.dot_general(ids, spread, (((0,), (0,)), ((), ())), preferred_element_type=jnp.float32)
+    expert = lax.broadcasted_iota(jnp.int32, (EXPERTS, LANES), 0).astype(jnp.float32)
+    chosen = jnp.zeros((EXPERTS, LANES), jnp.float32)
+    for choice in range(TOPK):
+        chosen = jnp.where(expert == named[choice : choice + 1, :], 1.0, chosen)
+    from_lane = lax.broadcasted_iota(jnp.int32, (LANES, LANES), 0)
+    to_lane = lax.broadcasted_iota(jnp.int32, (LANES, LANES), 1)
+    earlier = (from_lane // ROW_BLOCK == to_lane // ROW_BLOCK) & (from_lane < to_lane)
+    rank = jnp.dot(
+        chosen.astype(jnp.bfloat16), earlier.astype(jnp.float32).astype(jnp.bfloat16),
+        preferred_element_type=jnp.float32,
+    )
+    first_ref[...] = jnp.where(rank == 0.0, chosen, 0.0)
+    second_ref[...] = jnp.where(rank == 1.0, chosen, 0.0)
+    for tile in range(8):
+        for group in range(GROUPS):
+            column = (group * 8 + tile) * LANES
+            stack_ref[tile * 16 : (tile + 1) * 16, group * LANES : (group + 1) * LANES] = x_ref[
+                :, column : column + LANES
+            ]
+    sub = lax.broadcasted_iota(jnp.int32, (16, LANES), 0)
+    sub_lane = lax.broadcasted_iota(jnp.int32, (16, LANES), 1)
+    own_tile = sub_lane // ROW_BLOCK == sub // 2
+    mask_first = jnp.where(own_tile & (sub % 2 == 0), 1.0, 0.0)
+    mask_second = jnp.where(own_tile & (sub % 2 == 1), 1.0, 0.0)
+    stacked = stack_ref[...]
+    copies = []
+    per_piece = EXPERTS // PREP_PIECES
+    for piece in range(PREP_PIECES):
+        pieces = []
+        for expert_at in range(piece * per_piece, (piece + 1) * per_piece):
+            one = first_ref[expert_at : expert_at + 1, :]
+            two = second_ref[expert_at : expert_at + 1, :]
+            pieces.append((one * mask_first + two * mask_second).astype(jnp.bfloat16))
+        picker = jnp.concatenate(pieces, axis=0)
+        rows = jnp.dot(picker, stacked, preferred_element_type=jnp.float32).astype(jnp.bfloat16)
+        for group in range(GROUPS):
+            out_ref[
+                piece * per_piece : (piece + 1) * per_piece, group * 16 : (group + 1) * 16, :
+            ] = rows[:, group * LANES : (group + 1) * LANES].reshape(per_piece, 16, LANES)
+
+
+def weight_table_kernel(ids_ref, scores_ref, table_ref):
+    scores = scores_ref[...]
+    shares = scores / jnp.sum(scores, axis=1, keepdims=True)
+    ids = ids_ref[...]
+    expert = lax.broadcasted_iota(jnp.int32, (ROW_BLOCK, EXPERTS), 1)
+    chosen = jnp.zeros((ROW_BLOCK, EXPERTS), jnp.float32)
+    share_of = jnp.zeros((ROW_BLOCK, EXPERTS), jnp.float32)
+    for choice in range(TOPK):
+        same = ids[:, choice : choice + 1] == expert
+        chosen = jnp.where(same, 1.0, chosen)
+        share_of = jnp.where(same, shares[:, choice : choice + 1], share_of)
+    below = lax.broadcasted_iota(jnp.int32, (ROW_BLOCK, ROW_BLOCK), 1)
+    above = lax.broadcasted_iota(jnp.int32, (ROW_BLOCK, ROW_BLOCK), 0)
+    earlier = jnp.where(below < above, 1.0, 0.0).astype(jnp.bfloat16)
+    rank = jnp.dot(earlier, chosen.astype(jnp.bfloat16), preferred_element_type=jnp.float32)
+    slot_shares = jnp.concatenate(
+        [jnp.where(rank == 0.0, share_of, 0.0), jnp.where(rank == 1.0, share_of, 0.0)], axis=1
+    )
+    high = slot_shares.astype(jnp.bfloat16)
+    low = (slot_shares - high.astype(jnp.float32)).astype(jnp.bfloat16)
+    both = jnp.concatenate([high, low], axis=0)
+    piece = 512
+    for start in range(0, EXPERTS * 16, piece):
+        source = lax.broadcasted_iota(jnp.int32, (2 * EXPERTS, piece), 0)
+        target = lax.broadcasted_iota(jnp.int32, (2 * EXPERTS, piece), 1) + start
+        wanted = (target % 2) * EXPERTS + target // 16
+        spread = jnp.where(source == wanted, 1.0, 0.0).astype(jnp.bfloat16)
+        wide = jnp.dot(both, spread, preferred_element_type=jnp.float32)
+        tile_of = (lax.broadcasted_iota(jnp.int32, (ROW_BLOCK, piece), 1) // 2) % 8
+        for part in range(2):
+            rows = wide[part * ROW_BLOCK : (part + 1) * ROW_BLOCK, :]
+            for tile in range(8):
+                at = part * LANES + tile * ROW_BLOCK
+                table_ref[at : at + ROW_BLOCK, start : start + piece] = jnp.where(
+                    tile_of == tile, rows, 0.0
+                ).astype(jnp.bfloat16)
+
+
+def ffn_kernel(
+    x_hbm, gate_hbm, up_hbm, down_hbm, out_hbm,
+    x_ref, gate_ref, up_ref, down_ref, y_ref, rows_ref, gate_acc, up_acc, x_sem, gate_sem, up_sem, down_sem, y_sem,
+):
+    span = DMODEL // GROUPS
+
+    def x_copy(group):
+        return pltpu.make_async_copy(
+            x_hbm.at[:, pl.ds(group * 16, 16), :], x_ref.at[group], x_sem.at[group]
+        )
+
+    def gate_copy(group):
+        part = pl.ds(group * span, span)
+        return pltpu.make_async_copy(gate_hbm.at[0, part, :], gate_ref.at[part, :], gate_sem.at[group])
+
+    def up_copy(group):
+        part = pl.ds(group * span, span)
+        return pltpu.make_async_copy(up_hbm.at[0, part, :], up_ref.at[part, :], up_sem.at[group])
+
+    def down_copy(group):
+        part = pl.ds(group * span, span)
+        return pltpu.make_async_copy(down_hbm.at[0, :, part], down_ref.at[group], down_sem.at[group])
+
+    def y_copy(group):
+        return pltpu.make_async_copy(
+            y_ref.at[group], out_hbm.at[:, pl.ds(group * 16, 16), :], y_sem.at[group]
+        )
+
+    for group in range(GROUPS):
+        x_copy(group).start()
+        gate_copy(group).start()
+        up_copy(group).start()
+    for group in range(GROUPS):
+        down_copy(group).start()
+
+    out_row = lax.broadcasted_iota(jnp.int32, (LANES, LANES), 0)
+    in_row = lax.broadcasted_iota(jnp.int32, (LANES, LANES), 1)
+    gathered_from = (out_row // 2 % 8) * 16 + (out_row // 16) * 2 + out_row % 2
+    swap = jnp.where(in_row == gathered_from, 1.0, 0.0).astype(jnp.bfloat16)
+
+    for group in range(GROUPS):
+        x_copy(group).wait()
+        for block in range(0, 16, 2):
+            pair = jnp.concatenate(
+                [x_ref[group, (block + i) * 8 : (block + i + 1) * 8].reshape(LANES, LANES) for i in range(2)], axis=1
+            )
+            moved = jnp.dot(swap, pair, preferred_element_type=jnp.float32).astype(jnp.bfloat16)
+            for tile in range(8):
+                for i in range(2):
+                    rows_ref[
+                        (block + i) * 16 : (block + i + 1) * 16, tile * LANES : (tile + 1) * LANES
+                    ] = moved[tile * 16 : (tile + 1) * 16, i * LANES : (i + 1) * LANES]
+        rows = rows_ref[...]
+        gate_copy(group).wait()
+        gate_part = jnp.dot(
+            rows, gate_ref[group * span : (group + 1) * span, :], preferred_element_type=jnp.float32
+        )
+        up_copy(group).wait()
+        up_part = jnp.dot(
+            rows, up_ref[group * span : (group + 1) * span, :], preferred_element_type=jnp.float32
+        )
+        if group == 0:
+            gate_acc[...] = gate_part
+            up_acc[...] = up_part
+        else:
+            gate_acc[...] += gate_part
+            up_acc[...] += up_part
+    gate = gate_acc[...]
+    hidden = (gate / (1.0 + jnp.exp(-gate)) * up_acc[...]).astype(jnp.bfloat16)
+    for group in range(GROUPS):
+        down_copy(group).wait()
+        rows_ref[...] = jnp.dot(hidden, down_ref[group], preferred_element_type=jnp.float32).astype(jnp.bfloat16)
+        for block in range(0, 16, 2):
+            pair = jnp.concatenate(
+                [
+                    jnp.concatenate(
+                        [
+                            rows_ref[(block + i) * 16 : (block + i + 1) * 16, tile * LANES : (tile + 1) * LANES]
+                            for tile in range(8)
+                        ],
+                        axis=0,
+                    )
+                    for i in range(2)
+                ],
+                axis=1,
+            )
+            moved = jnp.dot(swap, pair, preferred_element_type=jnp.float32).astype(jnp.bfloat16)
+            for i in range(2):
+                y_ref[group, (block + i) * 8 : (block + i + 1) * 8] = moved[
+                    :, i * LANES : (i + 1) * LANES
+                ].reshape(8, 16, LANES)
+        y_copy(group).start()
+    for group in range(GROUPS):
+        y_copy(group).wait()
+
+
+def combine_kernel(table_ref, back_ref, out_ref, total_ref):
+    step = pl.program_id(0)
+    depth = back_ref.shape[0] * 16
+    part = jnp.dot(
+        table_ref[...],
+        jnp.concatenate(
+            [back_ref[:, group * 16 : (group + 1) * 16, :].reshape(depth, LANES) for group in range(GROUPS)], axis=1
+        ),
+        preferred_element_type=jnp.float32,
+    )
+
+    @pl.when(step == 0)
+    def _():
+        total_ref[...] = part
+
+    @pl.when(step > 0)
+    def _():
+        total_ref[...] += part
+
+    @pl.when(step == pl.num_programs(0) - 1)
+    def _():
+        summed = total_ref[:LANES, :] + total_ref[LANES:, :]
+        for tile in range(8):
+            for group in range(GROUPS):
+                column = (group * 8 + tile) * LANES
+                out_ref[:, column : column + LANES] = summed[
+                    tile * 16 : (tile + 1) * 16, group * LANES : (group + 1) * LANES
+                ].astype(jnp.bfloat16)
+
+
+def whole():
+    return pl.BlockSpec(memory_space=pltpu.VMEM)
+
+
+def cost(flops, moved):
+    return pl.CostEstimate(flops=flops, bytes_accessed=moved, transcendentals=0)
+
+
+def experts_of(moe_input, expert_ids, route_scores, w_gate, w_up, w_down):
+    exchange = jax.ShapeDtypeStruct((EXPERTS, CHUNK, LANES), jnp.bfloat16)
+    outgoing = pl.pallas_call(
+        slot_index_kernel,
+        out_shape=exchange,
+        in_specs=[whole(), whole()],
+        out_specs=whole(),
+        scratch_shapes=[
+            pltpu.VMEM((LANES, GROUPS * LANES), jnp.bfloat16),
+            pltpu.VMEM((EXPERTS, LANES), jnp.float32),
+            pltpu.VMEM((EXPERTS, LANES), jnp.float32),
+            pltpu.SemaphoreType.DMA((PREP_PIECES,)),
+        ],
+        compiler_params=pltpu.CompilerParams(vmem_limit_bytes=32 << 20),
+        cost_estimate=cost(300_000_000, 2_300_000),
+        name="dispatch_rows",
+    )(expert_ids, moe_input)
+    arrived = lax.all_to_all(outgoing, ("grp", "dev"), split_axis=0, concat_axis=0, tiled=True)
+    table = pl.pallas_call(
+        weight_table_kernel,
+        out_shape=jax.ShapeDtypeStruct((2 * LANES, EXPERTS * 16), jnp.bfloat16),
+        in_specs=[whole(), whole()],
+        out_specs=whole(),
+        compiler_params=pltpu.CompilerParams(vmem_limit_bytes=32 << 20),
+        cost_estimate=cost(100_000_000, 1_100_000),
+        name="route_table",
+    )(expert_ids, route_scores)
+    anywhere = pl.BlockSpec(memory_space=pl.ANY)
+    answers = pl.pallas_call(
+        ffn_kernel,
+        out_shape=exchange,
+        in_specs=[anywhere] * 4,
+        out_specs=anywhere,
+        scratch_shapes=[
+            pltpu.VMEM((GROUPS, EXPERTS, 16, LANES), jnp.bfloat16),
+            pltpu.VMEM((DMODEL, FF), jnp.bfloat16),
+            pltpu.VMEM((DMODEL, FF), jnp.bfloat16),
+            pltpu.VMEM((GROUPS, FF, DMODEL // GROUPS), jnp.bfloat16),
+            pltpu.VMEM((GROUPS, EXPERTS, 16, LANES), jnp.bfloat16),
+            pltpu.VMEM((2 * EXPERTS, DMODEL // GROUPS), jnp.bfloat16),
+            pltpu.VMEM((2 * EXPERTS, FF), jnp.float32),
+            pltpu.VMEM((2 * EXPERTS, FF), jnp.float32),
+        ]
+        + [pltpu.SemaphoreType.DMA((GROUPS,))] * 5,
+        compiler_params=pltpu.CompilerParams(vmem_limit_bytes=48 << 20),
+        cost_estimate=cost(4_800_000_000, 23_000_000),
+        name="expert_ffn",
+    )(arrived, w_gate, w_up, w_down)
+    returned = lax.all_to_all(answers, ("grp", "dev"), split_axis=0, concat_axis=0, tiled=True)
+    per_step = EXPERTS // COMBINE_STEPS
+    return pl.pallas_call(
+        combine_kernel,
+        grid=(COMBINE_STEPS,),
+        out_shape=jax.ShapeDtypeStruct((ROW_BLOCK, DMODEL), jnp.bfloat16),
+        in_specs=[
+            pl.BlockSpec((2 * LANES, per_step * 16), lambda step: (0, step)),
+            pl.BlockSpec((per_step, CHUNK, LANES), lambda step: (step, 0, 0)),
+        ],
+        out_specs=pl.BlockSpec((ROW_BLOCK, DMODEL), lambda step: (0, 0)),
+        scratch_shapes=[pltpu.VMEM((2 * LANES, GROUPS * LANES), jnp.float32)],
+        compiler_params=pltpu.CompilerParams(vmem_limit_bytes=32 << 20),
+        cost_estimate=cost(540_000_000, 3_300_000),
+        name="weighted_sum",
+    )(table, returned)
 
 
 def body(
@@ -77,39 +374,7 @@
     far_keys, far_values, far_len = partner((ext_keys, ext_values, ext_len), "dev", 0)
     far_part = partial_softmax(queries, far_keys, far_values, far_positions < far_len[:, None])
     attention_out = merge_parts(own_part, far_part)
-    devices = lax.axis_size("grp") * lax.axis_size("dev")
-    local_experts = w_gate.shape[0]
-    experts = devices * local_experts
-    row_count, top_count = expert_ids.shape
-    capacity = max(2, 2 * row_count * top_count // experts)
-    flat_ids = expert_ids.reshape(-1)
-    onehot = (flat_ids[:, None] == jnp.arange(experts, dtype=jnp.int32)[None, :]).astype(jnp.int32)
-    slot_rank = jnp.sum(jnp.cumsum(onehot, axis=0) * onehot, axis=1) - 1
-    slot_of = flat_ids * capacity + slot_rank
-    assign_rows = jnp.arange(row_count * top_count, dtype=jnp.int32) // top_count
-    sources = jnp.full((experts * capacity,), row_count, jnp.int32).at[slot_of].set(assign_rows)
-    padded = jnp.concatenate(
-        [moe_input, jnp.zeros((1, moe_input.shape[1]), moe_input.dtype)], axis=0
-    )
-    outgoing = padded[sources].reshape(devices, local_experts, capacity, -1)
-    arrived = lax.all_to_all(outgoing, ("grp", "dev"), split_axis=0, concat_axis=0, tiled=True)
-    gate_act = jnp.einsum("necd,edf->necf", arrived, w_gate, preferred_element_type=jnp.float32)
-    up_act = jnp.einsum("necd,edf->necf", arrived, w_up, preferred_element_type=jnp.float32)
-    hidden = (jax.nn.silu(gate_act) * up_act).astype(jnp.bfloat16)
-    returned = lax.all_to_all(
-        jnp.einsum("necf,efd->necd", hidden, w_down, preferred_element_type=jnp.float32).astype(
-            jnp.bfloat16
-        ),
-        ("grp", "dev"),
-        split_axis=0,
-        concat_axis=0,
-        tiled=True,
-    )
-    picked = returned.reshape(experts * capacity, -1)[slot_of].reshape(row_count, top_count, -1)
-    route_weights = route_scores / jnp.sum(route_scores, axis=1, keepdims=True)
-    moe_out = jnp.sum(route_weights[:, :, None] * picked.astype(jnp.float32), axis=1).astype(
-        jnp.bfloat16
-    )
+    moe_out = experts_of(moe_input, expert_ids, route_scores, w_gate, w_up, w_down)
     return (attention_out, moe_out)
 
 

time: 123 us -> 106 us (0.86)
  matrix products: 26 us -> 7.57 us
  Pallas kernels: 0 us -> 16.7 us
  local copies, waits for them, and re-layouts: 21.6 us -> 9.65 us
  other arithmetic: 6.97 us -> 4.82 us
  starting transfers between devices: 21.3 us -> 20 us
    dot_general x2 -> x0, matrix products: 18.4 us -> none  [the longest x1 12 us: body(): jnp.einsum('necf,efd->necd', hidden, w_down, preferred_element_type=jnp.f...]
    pallas_call x0 -> x4, Pallas kernels: none -> 16.7 us  [the longest x1 11.6 us: experts_of(): pl.pallas_call(ffn_kernel, out_shape=exchange, in_specs=[anywhere] * 4, o...]
    ppermute x3, waiting for transfers between devices: 0.01 us -> 9 us  [partner(): return lax.ppermute(block, axis, route)]
    all_to_all x2, waiting for transfers between devices: 45.3 us -> 37.2 us  [the longest x1 25.5 us: experts_of(): lax.all_to_all(answers, ('grp', 'dev'), split_axis=0, concat_axis=0, tile...]
    reshape x2 -> x0, local copies, waits for them, and re-layouts: 5.4 us -> none  [the longest x1 2.74 us: body(): returned.reshape(experts * capacity, -1)[slot_of]]
    convert_element_type x1 -> x0, local copies, waits for them, and re-layouts: 5.35 us -> none  [body(): jnp.einsum('necf,efd->necd', hidden, w_down, preferred_element_type=jnp.f...]
    unnamed x18 -> x25, local copies, waits for them, and re-layouts: 0.84 us -> 5.34 us
    gather x2 -> x0, local copies, waits for them, and re-layouts: 4.03 us -> none  [the longest x1 2.18 us: body(): returned.reshape(experts * capacity, -1)[slot_of]]
  transfers between devices with their start and end apart: 5 -> 5, of which waited for: 2 -> 3; matrix products, arithmetic and copies ran while one was open for 19% -> 17% of each run, Pallas kernels for 0% -> 3%
where the time goes in v1:
time: 106 us
  waiting for transfers between devices  46.2 us (44%)
  starting transfers between devices  20 us (19%)
  Pallas kernels  16.7 us (16%)
  local copies, waits for them, and re-layouts  9.65 us (9%)
  matrix products  7.57 us (7%)
  other arithmetic  4.82 us (5%)
    all_to_all x1, waiting for transfers between devices, experts_of(): lax.all_to_all(answers, ('grp', 'dev'), split_axis=0, concat_axis=0, tile...  25.5 us
    all_to_all x1, waiting for transfers between devices, experts_of(): lax.all_to_all(outgoing, ('grp', 'dev'), split_axis=0, concat_axis=0, til...  11.7 us
    pallas_call x1, Pallas kernels, experts_of(): pl.pallas_call(ffn_kernel, out_shape=exchange, in_specs=[anywhere] * 4, o...  11.6 us
    all_to_all x1, starting transfers between devices, experts_of(): lax.all_to_all(outgoing, ('grp', 'dev'), split_axis=0, concat_axis=0, til...  11.4 us
    ppermute x3, waiting for transfers between devices, partner(): return lax.ppermute(block, axis, route)  9 us
    all_to_all x1, starting transfers between devices, experts_of(): lax.all_to_all(answers, ('grp', 'dev'), split_axis=0, concat_axis=0, tile...  5.79 us
    unnamed x25, local copies, waits for them, and re-layouts  5.34 us
    dot_general x2, matrix products, partial_softmax(): numerator = jnp.einsum('rkgs,rskh->rkgh', weights, value_flat)  4.45 us
  transfers between devices with their start and end apart: 5, of which 3 were waited for; matrix products, arithmetic and copies ran while one was open for 17% of the time, Pallas kernels for 3%

profile of v1, /device:TPU:5, one launch (start us, length us, event | category | flops | bytes accessed | tf_op | source)
XLA Modules:
  0.0 105.7 jit_solution(9029141127889367037)
XLA Ops:
  0.6 0.0 copy-start
  0.6 1.4 %collective-permute-start = (s32[16]{0:T(128)}, s32[16]{0:T(128)}, u32[]{:S(2)}, u32[]{:S(2)}) collective-permute-start(s32[16]{0:T(128)} %param.21), channel_id=1, source_target_pairs={{0,1},{1,0},{2,3},{3,2},{4,5},{5,4},{6,7},{7,6},{8,9},{9,8},{10,11... | collective-permute-start | bytes 200 | tf_op jit(solution)/shard_map/ppermute | solution.py:30
  2.0 0.2 collective-permute-start.1
  2.2 1.3 %collective-permute-start.2 = (bf16[16,32,512]{2,1,0:T(8,128)(2,1)}, bf16[16,32,512]{2,1,0:T(8,128)(2,1)}, u32[]{:S(2)}, u32[]{:S(2)}) collective-permute-start(bf16[16,32,512]{2,1,0:T(8,128)(2,1)} %param.20), channel_id=1, source_target_pairs={{0,1},{1,0},{2,3},{3,2},{4,5},{5,4},{6,7},{7,6},{8,9},{9,8},{10,11... | collective-permute-start | bytes 1572872 | tf_op jit(solution)/shard_map/ppermute | solution.py:30
  3.5 0.8 copy.26.ids_ref
  4.2 0.0 copy-start.4
  4.2 0.9 copy-done.4
  5.2 2.4 %dispatch_rows.1 = bf16[128,64,128]{2,1,0:T(8,128)(2,1)} custom-call(s32[16,8]{1,0:T(8,128)S(1)} %copy.26.ids_ref, bf16[16,4096]{1,0:T(8,128)(2,1)S(1)} %copy-done.4), custom_call_target="tpu_custom_call" | custom-call | flops 300000000 | bytes 2300000 | tf_op jit(solution)/shard_map/dispatch_rows/pallas_call | solution.py:286
  7.5 0.0 copy-start.6
  7.5 0.0 copy-start.7
  7.5 0.0 copy-start.10
  7.6 11.4 %all-to-all-start = ((bf16[128,64,128]{2,1,0:T(8,128)(2,1)}), bf16[128,64,128]{2,1,0:T(8,128)(2,1)S(1)}, u32[]{:S(2)}, u32[]{:S(2)}) async-start(bf16[128,64,128]{2,1,0:T(8,128)(2,1)} %dispatch_rows.1), calls=%async_computation | async-start | bytes 4194304 | tf_op jit(solution)/shard_map/all_to_all | solution.py:301
  18.9 0.0 copy-done.6
  19.0 0.0 copy-done
  19.0 0.9 copy_bitcast_fusion.1
  19.9 0.0 copy-done.7
  19.9 0.0 copy-start.8
  19.9 0.0 copy-start.9
  20.0 0.0 copy-done.10
  20.0 0.1 fusion.24
  20.0 1.6 %select_reduce_fusion.1 = (f32[16,4,16]{2,1,0:T(4,128)S(1)}, f32[16,4,33,16]{2,3,1,0:T(8,128)S(1)}) fusion(pred[16,33]{1,0:T(8,128)(4,1)S(1)} %fusion.24, bf16[16,4,16,128]{3,2,1,0:T(8,128)(2,1)S(1)} %bitcast.62, bf16[16,1,4,128]{3,1,2,0:T(2,128)(2,1)S(1)} %concatenate.22, bf16[16,32,4,128]{3,1,2,0:T(8,128)(2,1)} %copy_bitcast_fusion.1), kind=kOutput, calls=%fused_computation.24 | convolution fusion | flops 9832448 | bytes 942608 | tf_op jit(solution)/shard_map/rkgh,rskh->rkgs/dot_general | solution.py:39
  21.6 0.5 slice_bitcast_fusion
  22.2 1.9 %copy_bitcast_fusion = bf16[16,32,4,128]{3,1,2,0:T(8,128)(2,1)} fusion(bf16[16,32,512]{2,1,0:T(8,128)(2,1)} %param.17), kind=kLoop, calls=%fused_computation.19 | loop fusion | bytes 1048576 | tf_op jit(solution)/shard_map/concatenate | solution.py:371
  24.1 0.4 fusion.14
  24.5 0.1 reduce_max.23
  24.6 0.0 copy-done.8
  24.7 0.0 copy-done.9
  24.7 0.1 copy.27.scores_ref
  24.7 0.5 route_table.1.table_ref
  25.3 0.0 copy-start.2
  25.3 1.0 copy-done.2
  26.3 2.3 %fusion.3 = f32[16,4,16,128]{3,2,1,0:T(8,128)} fusion(bf16[16,1,4,128]{3,1,2,0:T(2,128)(2,1)S(1)} %concatenate.23, bf16[16,32,4,128]{3,1,2,0:T(8,128)(2,1)} %copy_bitcast_fusion, f32[16,4,33,16]{2,3,1,0:T(8,128)S(1)} %get-tuple-element.8, f32[16,4,16]{2,1,0:T(4,128)S(1)} %is-finite_select_fusion.1, pred[16,33]{1,0:T(8,128)(4,1)S(1)} %fusion.24), kind=kOutput, calls=%fused_computation.5 | convolution fusion | flops 9799680 | bytes 1204752 | tf_op jit(solution)/shard_map/rkgs,rskh->rkgh/dot_general | solution.py:45
  28.5 0.1 reshape.169
  28.6 0.0 collective-permute-done
  28.6 0.7 broadcast_compare_fusion
  29.3 0.0 collective-permute-done.1
  29.3 1.5 %select_reduce_fusion = (f32[16,4,16]{2,1,0:T(4,128)S(1)}, f32[16,4,16,32]{3,2,1,0:T(8,128)S(1)}) fusion(pred[16,32]{1,0:T(8,128)(4,1)S(1)} %broadcast_compare_fusion, bf16[16,4,16,128]{3,2,1,0:T(8,128)(2,1)S(1)} %bitcast.63, bf16[16,32,512]{2,1,0:T(8,128)(2,1)} %collective-permute-done.1), kind=kOutput, calls=%fused_computation.22 | convolution fusion | flops 8485888 | bytes 922112 | tf_op jit(solution)/shard_map/rkgh,rskh->rkgs/dot_general | solution.py:39
  30.9 0.1 reduce_max.25
  31.0 0.4 fusion.15
  31.4 0.1 reshape.170
  31.5 9.0 %collective-permute-done.2 = bf16[16,32,512]{2,1,0:T(8,128)(2,1)} collective-permute-done((bf16[16,32,512]{2,1,0:T(8,128)(2,1)}, bf16[16,32,512]{2,1,0:T(8,128)(2,1)}, u32[]{:S(2)}, u32[]{:S(2)}) %collective-permute-start.2) | collective-permute-done | bytes 524320 | tf_op jit(solution)/shard_map/ppermute | solution.py:30
  40.5 2.2 %fusion.9 = f32[16,4,16,128]{3,2,1,0:T(8,128)} fusion(f32[16,4,16,32]{3,2,1,0:T(8,128)S(1)} %get-tuple-element.6, f32[16,4,16]{2,1,0:T(4,128)S(1)} %is-finite_select_fusion, pred[16,32]{1,0:T(8,128)(4,1)S(1)} %broadcast_compare_fusion, bf16[16,32,512]{2,1,0:T(8,128)(2,1)} %collective-permute-done.2), kind=kOutput, calls=%fused_computation.14 | convolution fusion | flops 8454144 | bytes 1184256 | tf_op jit(solution)/shard_map/rkgs,rskh->rkgh/dot_general | solution.py:45
  42.7 11.7 %all-to-all-done.x_hbm = bf16[128,64,128]{2,1,0:T(8,128)(2,1)S(1)} async-done(((bf16[128,64,128]{2,1,0:T(8,128)(2,1)}), bf16[128,64,128]{2,1,0:T(8,128)(2,1)S(1)}, u32[]{:S(2)}, u32[]{:S(2)}) %all-to-all-start) | async-done | bytes 2097184 | tf_op jit(solution)/shard_map/all_to_all | solution.py:301
  54.3 11.6 %expert_ffn.1 = bf16[128,64,128]{2,1,0:T(8,128)(2,1)S(1)} custom-call(bf16[128,64,128]{2,1,0:T(8,128)(2,1)S(1)} %all-to-all-done.x_hbm, bf16[1,4096,768]{2,1,0:T(8,128)(2,1)} %gate_hbm.1, bf16[1,4096,768]{2,1,0:T(8,128)(2,1)} %up_hbm.1, bf16[1,768,4096]{2,1,0:T(8,128)(2,1)} %down_hbm.1), custom_call_target="tpu_custom_call" | custom-call | flops 4800000000 | bytes 23000000 | tf_op jit(solution)/shard_map/expert_ffn/pallas_call | solution.py:312
  65.9 0.0 copy-start.1
  65.9 1.3 %copy-done.1 = bf16[128,64,128]{2,1,0:T(8,128)(2,1)} copy-done((bf16[128,64,128]{2,1,0:T(8,128)(2,1)}, bf16[128,64,128]{2,1,0:T(8,128)(2,1)S(1)}, u32[]{:S(2)}) %copy-start.1) | copy-done | bytes 2097176
  67.3 0.0 copy-start.5
  67.3 5.8 %all-to-all-start.1 = ((bf16[128,64,128]{2,1,0:T(8,128)(2,1)}), bf16[128,64,128]{2,1,0:T(8,128)(2,1)S(1)}, u32[]{:S(2)}, u32[]{:S(2)}) async-start(bf16[128,64,128]{2,1,0:T(8,128)(2,1)} %copy-done.1), calls=%async_computation.1 | async-start | bytes 4194304 | tf_op jit(solution)/shard_map/all_to_all | solution.py:332
  73.1 0.2 mul.36
  73.3 0.2 mul.39
  73.5 0.2 div.27
  73.7 0.0 copy-done.5
  73.7 3.1 %fusion.7 = bf16[16,8192]{1,0:T(8,128)(2,1)} fusion(f32[2,8,64,128]{3,2,1,0:T(8,128)S(1)} %bitcast.61, f32[2,8,64,128]{3,2,1,0:T(8,128)S(1)} %bitcast.60, f32[2,8,64,128]{3,2,1,0:T(8,128)S(1)} %bitcast.58, f32[2,8,64,128]{3,2,1,0:T(8,128)S(1)} %bitcast.59, f32[2,8,64,128]{3,2,1,0:T(8,128)} %bitcast.64), kind=kLoop, calls=%fused_computation.10 | loop fusion | flops 655360 | bytes 2883584 | tf_op jit(solution)/shard_map/convert_element_type | solution.py:62
  76.8 25.5 %all-to-all-done.1.back_ref = bf16[128,64,128]{2,1,0:T(8,128)(2,1)S(1)} async-done(((bf16[128,64,128]{2,1,0:T(8,128)(2,1)}), bf16[128,64,128]{2,1,0:T(8,128)(2,1)S(1)}, u32[]{:S(2)}, u32[]{:S(2)}) %all-to-all-start.1) | async-done | bytes 2097184 | tf_op jit(solution)/shard_map/all_to_all | solution.py:332
  102.3 0.0 copy-start.3
  102.3 1.2 %copy-done.3 = bf16[256,2048]{1,0:T(8,128)(2,1)S(1)} copy-done((bf16[256,2048]{1,0:T(8,128)(2,1)S(1)}, bf16[256,2048]{1,0:T(8,128)(2,1)}, u32[]{:S(2)}) %copy-start.3) | copy-done | bytes 1048600
  103.6 2.2 %weighted_sum.1 = bf16[16,4096]{1,0:T(8,128)(2,1)} custom-call(bf16[256,2048]{1,0:T(8,128)(2,1)S(1)} %copy-done.3, bf16[128,64,128]{2,1,0:T(8,128)(2,1)S(1)} %all-to-all-done.1.back_ref), custom_call_target="tpu_custom_call" | custom-call | flops 540000000 | bytes 3300000 | tf_op jit(solution)/shard_map/weighted_sum/pallas_call | solution.py:334
  (8 shorter events, 0.1 us)
Async XLA Ops:
  0.6 18.4 %copy-start = (bf16[16,32,512]{2,1,0:T(8,128)(2,1)S(1)}, bf16[16,32,512]{2,1,0:T(8,128)(2,1)}, u32[]{:S(2)}) copy-start(bf16[16,32,512]{2,1,0:T(8,128)(2,1)} %param.16) | copy-start | bytes 1572868
  0.6 28.0 %collective-permute-start = (s32[16]{0:T(128)}, s32[16]{0:T(128)}, u32[]{:S(2)}, u32[]{:S(2)}) collective-permute-start(s32[16]{0:T(128)} %param.21), channel_id=1, source_target_pairs={{0,1},{1,0},{2,3},{3,2},{4,5},{5,4},{6,7},{7,6},{8,9},{9,8},{10,11... | collective-permute-start | bytes 200 | tf_op jit(solution)/shard_map/ppermute | solution.py:30
  2.0 27.3 %collective-permute-start.1 = (bf16[16,32,512]{2,1,0:T(8,128)(2,1)}, bf16[16,32,512]{2,1,0:T(8,128)(2,1)}, u32[]{:S(2)}, u32[]{:S(2)}) collective-permute-start(bf16[16,32,512]{2,1,0:T(8,128)(2,1)} %param.19), channel_id=1, source_target_pairs={{0,1},{1,0},{2,3},{3,2},{4,5},{5,4},{6,7},{7,6},{8,9},{9,8},{10,11... | collective-permute-start | bytes 1572872 | tf_op jit(solution)/shard_map/ppermute | solution.py:30
  2.2 38.3 %collective-permute-start.2 = (bf16[16,32,512]{2,1,0:T(8,128)(2,1)}, bf16[16,32,512]{2,1,0:T(8,128)(2,1)}, u32[]{:S(2)}, u32[]{:S(2)}) collective-permute-start(bf16[16,32,512]{2,1,0:T(8,128)(2,1)} %param.20), channel_id=1, source_target_pairs={{0,1},{1,0},{2,3},{3,2},{4,5},{5,4},{6,7},{7,6},{8,9},{9,8},{10,11... | collective-permute-start | bytes 1572872 | tf_op jit(solution)/shard_map/ppermute | solution.py:30
  4.2 0.9 copy-start.4
  7.5 11.4 %copy-start.6 = (bf16[16,8192]{1,0:T(8,128)(2,1)S(1)}, bf16[16,8192]{1,0:T(8,128)(2,1)}, u32[]{:S(2)}) copy-start(bf16[16,8192]{1,0:T(8,128)(2,1)} %param.15) | copy-start | bytes 786436
  7.5 12.4 %copy-start.7 = (bf16[16,512]{1,0:T(8,128)(2,1)S(1)}, bf16[16,512]{1,0:T(8,128)(2,1)}, u32[]{:S(2)}) copy-start(bf16[16,512]{1,0:T(8,128)(2,1)} %param.22) | copy-start | bytes 49156
  7.5 12.4 %copy-start.10 = (s32[16]{0:T(128)S(1)}, s32[16]{0:T(128)}, u32[]{:S(2)}) copy-start(s32[16]{0:T(128)} %param.18) | copy-start | bytes 196
  7.6 46.8 %all-to-all-start = ((bf16[128,64,128]{2,1,0:T(8,128)(2,1)}), bf16[128,64,128]{2,1,0:T(8,128)(2,1)S(1)}, u32[]{:S(2)}, u32[]{:S(2)}) async-start(bf16[128,64,128]{2,1,0:T(8,128)(2,1)} %dispatch_rows.1), calls=%async_computation | async-start | bytes 4194304 | tf_op jit(solution)/shard_map/all_to_all | solution.py:301
  19.9 4.7 %copy-start.8 = (bf16[16,512]{1,0:T(8,128)(2,1)S(1)}, bf16[16,512]{1,0:T(8,128)(2,1)}, u32[]{:S(2)}) copy-start(bf16[16,512]{1,0:T(8,128)(2,1)} %param.23) | copy-start | bytes 49156
  19.9 4.7 %copy-start.9 = (f32[16,8]{0,1:T(8,128)S(1)}, f32[16,8]{0,1:T(8,128)}, u32[]{:S(2)}) copy-start(f32[16,8]{0,1:T(8,128)} %param.26) | copy-start | bytes 1540
  25.3 1.0 copy-start.2
  65.9 1.3 %copy-start.1 = (bf16[128,64,128]{2,1,0:T(8,128)(2,1)}, bf16[128,64,128]{2,1,0:T(8,128)(2,1)S(1)}, u32[]{:S(2)}) copy-start(bf16[128,64,128]{2,1,0:T(8,128)(2,1)S(1)} %expert_ffn.1) | copy-start | bytes 6291460
  67.3 6.4 %copy-start.5 = (f32[16,4,16,128]{3,2,1,0:T(8,128)S(1)}, f32[16,4,16,128]{3,2,1,0:T(8,128)}, u32[]{:S(2)}) copy-start(f32[16,4,16,128]{3,2,1,0:T(8,128)} %fusion.9) | copy-start | bytes 1572868
  67.3 35.1 %all-to-all-start.1 = ((bf16[128,64,128]{2,1,0:T(8,128)(2,1)}), bf16[128,64,128]{2,1,0:T(8,128)(2,1)S(1)}, u32[]{:S(2)}, u32[]{:S(2)}) async-start(bf16[128,64,128]{2,1,0:T(8,128)(2,1)} %copy-done.1), calls=%async_computation.1 | async-start | bytes 4194304 | tf_op jit(solution)/shard_map/all_to_all | solution.py:332
  102.3 1.2 %copy-start.3 = (bf16[256,2048]{1,0:T(8,128)(2,1)S(1)}, bf16[256,2048]{1,0:T(8,128)(2,1)}, u32[]{:S(2)}) copy-start(bf16[256,2048]{1,0:T(8,128)(2,1)} %copy-done.2) | copy-start | bytes 3145732

commit v2 on v1

v2 whole, which is shorter than its diff:
```python
import jax
import jax.numpy as jnp
from jax import lax
from jax.experimental import pallas as pl
from jax.experimental.pallas import tpu as pltpu
from jax.sharding import PartitionSpec as P

QH = 64
KVH = 4
HD = 128
DMODEL = 4096
FF = 768
TOPK = 8
EXPERTS = 128
ROW_BLOCK = 16
LANES = 128
GROUPS = 4
CHUNK = 64
PREP_PIECES = 8
FFN_PIECES = 8
FFN_AHEAD = 3
ALL_VMEM = 60 << 20
FFN_VMEM = 48 << 20
TIE_VMEM = 16 << 20
LATE_TIE_VMEM = 16 << 20


def partner(block, axis, apart):
    count = lax.axis_size(axis)
    route = []
    for low in range(count):
        high = low | 1 << apart
        if high != low and high < count:
            route += [(low, high), (high, low)]
    return lax.ppermute(block, axis, route)


def partial_softmax(queries, keys, values, live_slots):
    row_count = queries.shape[0]
    groups = QH // KVH
    query_flat = queries.astype(jnp.float32).reshape(row_count, KVH, groups, HD)
    key_flat = keys.astype(jnp.float32).reshape(row_count, keys.shape[1], KVH, HD)
    value_flat = values.astype(jnp.float32).reshape(row_count, values.shape[1], KVH, HD)
    scores = jnp.einsum("rkgh,rskh->rkgs", query_flat, key_flat) / jnp.sqrt(jnp.float32(HD))
    live_mask = live_slots[:, None, None, :]
    row_max = jnp.max(jnp.where(live_mask, scores, -jnp.inf), axis=-1)
    row_max = jnp.where(jnp.isfinite(row_max), row_max, -1e30)
    weights = jnp.where(live_mask, jnp.exp(scores - row_max[..., None]), 0.0)
    row_total = jnp.sum(weights, axis=-1)
    numerator = jnp.einsum("rkgs,rskh->rkgh", weights, value_flat)
    return (
        row_max.reshape(row_count, QH),
        row_total.reshape(row_count, QH),
        numerator.reshape(row_count, QH, HD),
    )


def packed_part(part):
    row_max, row_total, numerator = part
    live = row_total > 0.0
    safe = jnp.where(live, row_total, 1.0)
    level = jnp.where(live, row_max + jnp.log(safe), -1e30)
    high = lax.reduce_precision(level, 8, 7)
    middle = lax.reduce_precision(level - high, 8, 7)
    low = level - high - middle
    levels = jnp.concatenate([high, middle, low, jnp.zeros_like(low)], axis=1)
    mean = numerator / safe[..., None]
    return jnp.concatenate([mean, levels.reshape(-1, 2, HD)], axis=1).astype(jnp.bfloat16)


def unpacked_part(packed):
    levels = packed[:, QH:].reshape(-1, 4, QH).astype(jnp.float32)
    return levels[:, 0] + levels[:, 1] + levels[:, 2], packed[:, :QH]


def tie_kernel(one_ref, two_ref, one_out_ref, two_out_ref):
    pass


def tied(one, two, limit):
    anywhere = pl.BlockSpec(memory_space=pl.ANY)
    return pl.pallas_call(
        tie_kernel,
        out_shape=[jax.ShapeDtypeStruct(kept.shape, kept.dtype) for kept in (one, two)],
        in_specs=[anywhere, anywhere],
        out_specs=[anywhere, anywhere],
        input_output_aliases={0: 0, 1: 1},
        compiler_params=pltpu.CompilerParams(vmem_limit_bytes=limit),
        cost_estimate=cost(0, 0),
        name="order",
    )(one, two)


def merge_parts(first, second):
    max_one, total_one, numer_one = first
    level_two, mean_two = second
    largest = jnp.maximum(max_one, level_two)
    scale_one = jnp.exp(max_one - largest)
    scale_two = jnp.exp(level_two - largest)
    row_total = total_one * scale_one + scale_two
    numerator = numer_one * scale_one[..., None] + mean_two.astype(jnp.float32) * scale_two[..., None]
    merged = numerator / row_total[..., None]
    return merged.reshape(merged.shape[0], -1).astype(jnp.bfloat16)


def dispatch_kernel(
    ids_hbm, x_hbm, out_hbm, ids_ref, x_ref, stack_ref, first_ref, second_ref, out_ref, ids_sem, x_sem, out_sem
):
    ids_copy = pltpu.make_async_copy(ids_hbm, ids_ref, ids_sem)
    ids_copy.start()
    x_copy = pltpu.make_async_copy(x_hbm, x_ref, x_sem)
    x_copy.start()
    lane = lax.broadcasted_iota(jnp.int32, (ROW_BLOCK, LANES), 1)
    row = lax.broadcasted_iota(jnp.int32, (ROW_BLOCK, LANES), 0)
    spread = jnp.where(lane % ROW_BLOCK == row, 1.0, 0.0).astype(jnp.bfloat16)
    expert = lax.broadcasted_iota(jnp.int32, (EXPERTS, LANES), 0).astype(jnp.float32)
    ids_copy.wait()
    ids = ids_ref[...].astype(jnp.float32).astype(jnp.bfloat16)
    named = jnp.dot(ids, spread, preferred_element_type=jnp.float32)
    chosen = jnp.zeros((EXPERTS, LANES), jnp.float32)
    for choice in range(TOPK):
        chosen = jnp.where(expert == named[choice : choice + 1, :], 1.0, chosen)
    from_lane = lax.broadcasted_iota(jnp.int32, (LANES, LANES), 0)
    to_lane = lax.broadcasted_iota(jnp.int32, (LANES, LANES), 1)
    earlier = (from_lane // ROW_BLOCK == to_lane // ROW_BLOCK) & (from_lane < to_lane)
    rank = jnp.dot(
        chosen.astype(jnp.bfloat16),
        jnp.where(earlier, 1.0, 0.0).astype(jnp.bfloat16),
        preferred_element_type=jnp.float32,
    )
    first_ref[...] = jnp.where(rank == 0.0, chosen, 0.0)
    second_ref[...] = jnp.where(rank == 1.0, chosen, 0.0)
    sub = lax.broadcasted_iota(jnp.int32, (16, LANES), 0)
    sub_lane = lax.broadcasted_iota(jnp.int32, (16, LANES), 1)
    own_tile = sub_lane // ROW_BLOCK == sub // 2
    mask_first = jnp.where(own_tile & (sub % 2 == 0), 1.0, 0.0)
    mask_second = jnp.where(own_tile & (sub % 2 == 1), 1.0, 0.0)
    x_copy.wait()
    for tile in range(8):
        for group in range(GROUPS):
            column = (group * 8 + tile) * LANES
            stack_ref[tile * 16 : (tile + 1) * 16, group * LANES : (group + 1) * LANES] = x_ref[
                :, column : column + LANES
            ]
    stacked = stack_ref[...]
    per_piece = EXPERTS // PREP_PIECES

    def out_copy(piece):
        part = pl.ds(piece * per_piece, per_piece)
        return pltpu.make_async_copy(out_ref.at[part], out_hbm.at[part], out_sem.at[piece])

    for piece in range(PREP_PIECES):
        pickers = []
        for expert_at in range(piece * per_piece, (piece + 1) * per_piece):
            one = first_ref[expert_at : expert_at + 1, :]
            two = second_ref[expert_at : expert_at + 1, :]
            pickers.append((one * mask_first + two * mask_second).astype(jnp.bfloat16))
        picker = jnp.concatenate(pickers, axis=0)
        rows = jnp.dot(picker, stacked, preferred_element_type=jnp.float32).astype(jnp.bfloat16)
        for group in range(GROUPS):
            out_ref[
                piece * per_piece : (piece + 1) * per_piece, group * 16 : (group + 1) * 16, :
            ] = rows[:, group * LANES : (group + 1) * LANES].reshape(per_piece, 16, LANES)
        out_copy(piece).start()
    for piece in range(PREP_PIECES):
        out_copy(piece).wait()


def slot_shares_kernel(ids_ref, scores_ref, shares_ref):
    scores = scores_ref[...]
    shares = scores / jnp.sum(scores, axis=1, keepdims=True)
    ids = ids_ref[...]
    expert = lax.broadcasted_iota(jnp.int32, (ROW_BLOCK, EXPERTS), 1)
    chosen = jnp.zeros((ROW_BLOCK, EXPERTS), jnp.float32)
    share_of = jnp.zeros((ROW_BLOCK, EXPERTS), jnp.float32)
    for choice in range(TOPK):
        same = ids[:, choice : choice + 1] == expert
        chosen = jnp.where(same, 1.0, chosen)
        share_of = jnp.where(same, shares[:, choice : choice + 1], share_of)
    below = lax.broadcasted_iota(jnp.int32, (ROW_BLOCK, ROW_BLOCK), 1)
    above = lax.broadcasted_iota(jnp.int32, (ROW_BLOCK, ROW_BLOCK), 0)
    earlier = jnp.where(below < above, 1.0, 0.0).astype(jnp.bfloat16)
    rank = jnp.dot(earlier, chosen.astype(jnp.bfloat16), preferred_element_type=jnp.float32)
    slot_shares = jnp.concatenate(
        [jnp.where(rank == 0.0, share_of, 0.0), jnp.where(rank == 1.0, share_of, 0.0)], axis=1
    )
    high = slot_shares.astype(jnp.bfloat16)
    low = (slot_shares - high.astype(jnp.float32)).astype(jnp.bfloat16)
    shares_ref[...] = jnp.concatenate([high, low], axis=0)


def ffn_kernel(
    x_ref, gate_hbm, up_hbm, down_hbm, old_hbm, out_hbm,
    gate_ref, up_ref, down_ref, y_ref, rows_ref, in_sem, y_sem,
):
    span = DMODEL // GROUPS
    deep = DMODEL // FFN_PIECES

    def first_copies(piece):
        part = pl.ds(piece * deep, deep)
        return [
            pltpu.make_async_copy(gate_hbm.at[0, part, :], gate_ref.at[part, :], in_sem.at[0, piece]),
            pltpu.make_async_copy(up_hbm.at[0, part, :], up_ref.at[part, :], in_sem.at[1, piece]),
        ]

    def second_copies(piece):
        part = pl.ds(piece * deep, deep)
        return [pltpu.make_async_copy(down_hbm.at[0, :, part], down_ref.at[:, part], in_sem.at[2, piece])]

    queue = [first_copies(piece) for piece in range(FFN_PIECES)]
    queue += [second_copies(2 * pair) + second_copies(2 * pair + 1) for pair in range(FFN_PIECES // 2)]
    started = 0

    def start_until(count):
        nonlocal started
        while started < min(count, len(queue)):
            for copy in queue[started]:
                copy.start()
            started += 1

    def wait_for(index):
        for copy in queue[index]:
            copy.wait()
        start_until(index + 1 + FFN_AHEAD)

    def y_copy(group):
        return pltpu.make_async_copy(
            y_ref.at[group], out_hbm.at[:, pl.ds(group * 16, 16), :], y_sem.at[group]
        )

    start_until(FFN_AHEAD)
    out_row = lax.broadcasted_iota(jnp.int32, (LANES, LANES), 0)
    in_row = lax.broadcasted_iota(jnp.int32, (LANES, LANES), 1)
    gathered_from = (out_row // 2 % 8) * 16 + (out_row // 16) * 2 + out_row % 2
    swap = jnp.where(in_row == gathered_from, 1.0, 0.0).astype(jnp.bfloat16)

    for group in range(GROUPS):
        for block in range(0, 16, 2):
            pair = jnp.concatenate(
                [
                    x_ref[(block + i) * 8 : (block + i + 1) * 8, group * 16 : (group + 1) * 16].reshape(LANES, LANES)
                    for i in range(2)
                ],
                axis=1,
            )
            moved = jnp.dot(swap, pair, preferred_element_type=jnp.float32).astype(jnp.bfloat16)
            for tile in range(8):
                column = group * span + tile * LANES
                for i in range(2):
                    rows_ref[(block + i) * 16 : (block + i + 1) * 16, column : column + LANES] = moved[
                        tile * 16 : (tile + 1) * 16, i * LANES : (i + 1) * LANES
                    ]
    gate = up = None
    for piece in range(FFN_PIECES):
        wait_for(piece)
        part = slice(piece * deep, (piece + 1) * deep)
        rows = rows_ref[:, part]
        gate_part = jnp.dot(rows, gate_ref[part, :], preferred_element_type=jnp.float32)
        up_part = jnp.dot(rows, up_ref[part, :], preferred_element_type=jnp.float32)
        gate = gate_part if gate is None else gate + gate_part
        up = up_part if up is None else up + up_part
    hidden = (gate / (1.0 + jnp.exp(-gate)) * up).astype(jnp.bfloat16)
    for group in range(GROUPS):
        part = slice(group * span, (group + 1) * span)
        for piece in range(group * FFN_PIECES // 8, (group + 1) * FFN_PIECES // 8):
            wait_for(FFN_PIECES + piece)
        rows_ref[:, part] = jnp.dot(
            hidden, down_ref[:, part], preferred_element_type=jnp.float32
        ).astype(jnp.bfloat16)
        for block in range(0, 16, 2):
            pair = jnp.concatenate(
                [
                    jnp.concatenate(
                        [
                            rows_ref[
                                (block + i) * 16 : (block + i + 1) * 16,
                                group * span + tile * LANES : group * span + (tile + 1) * LANES,
                            ]
                            for tile in range(8)
                        ],
                        axis=0,
                    )
                    for i in range(2)
                ],
                axis=1,
            )
            moved = jnp.dot(swap, pair, preferred_element_type=jnp.float32).astype(jnp.bfloat16)
            for i in range(2):
                y_ref[group, (block + i) * 8 : (block + i + 1) * 8] = moved[
                    :, i * LANES : (i + 1) * LANES
                ].reshape(8, 16, LANES)
        y_copy(group).start()
    for group in range(GROUPS):
        y_copy(group).wait()


def combine_kernel(shares_ref, back_ref, out_ref, table_ref):
    both = shares_ref[...]
    piece = 512
    for start in range(0, EXPERTS * 16, piece):
        source = lax.broadcasted_iota(jnp.int32, (2 * EXPERTS, piece), 0)
        target = lax.broadcasted_iota(jnp.int32, (2 * EXPERTS, piece), 1) + start
        wanted = (target % 2) * EXPERTS + target // 16
        spread = jnp.where(source == wanted, 1.0, 0.0).astype(jnp.bfloat16)
        wide = jnp.dot(both, spread, preferred_element_type=jnp.float32)
        tile_of = (lax.broadcasted_iota(jnp.int32, (ROW_BLOCK, piece), 1) // 2) % 8
        for part in range(2):
            rows = wide[part * ROW_BLOCK : (part + 1) * ROW_BLOCK, :]
            for tile in range(8):
                at = part * LANES + tile * ROW_BLOCK
                table_ref[at : at + ROW_BLOCK, start : start + piece] = jnp.where(
                    tile_of == tile, rows, 0.0
                ).astype(jnp.bfloat16)
    back = jnp.concatenate(
        [
            back_ref[:, group * 16 : (group + 1) * 16, :].reshape(EXPERTS * 16, LANES)
            for group in range(GROUPS)
        ],
        axis=1,
    )
    total = jnp.dot(table_ref[...], back, preferred_element_type=jnp.float32)
    summed = total[:LANES, :] + total[LANES:, :]
    for tile in range(8):
        for group in range(GROUPS):
            column = (group * 8 + tile) * LANES
            out_ref[:, column : column + LANES] = summed[
                tile * 16 : (tile + 1) * 16, group * LANES : (group + 1) * LANES
            ].astype(jnp.bfloat16)


def whole():
    return pl.BlockSpec(memory_space=pltpu.VMEM)


def cost(flops, moved):
    return pl.CostEstimate(flops=flops, bytes_accessed=moved, transcendentals=0)


def dispatched(moe_input, expert_ids, route_scores):
    exchange = jax.ShapeDtypeStruct((EXPERTS, CHUNK, LANES), jnp.bfloat16)
    in_hbm = pl.BlockSpec(memory_space=pltpu.HBM)
    outgoing = pl.pallas_call(
        dispatch_kernel,
        out_shape=exchange,
        in_specs=[in_hbm, in_hbm],
        out_specs=in_hbm,
        scratch_shapes=[
            pltpu.VMEM((TOPK, ROW_BLOCK), jnp.int32),
            pltpu.VMEM((ROW_BLOCK, DMODEL), jnp.bfloat16),
            pltpu.VMEM((LANES, GROUPS * LANES), jnp.bfloat16),
            pltpu.VMEM((EXPERTS, LANES), jnp.float32),
            pltpu.VMEM((EXPERTS, LANES), jnp.float32),
            pltpu.VMEM((EXPERTS, CHUNK, LANES), jnp.bfloat16),
            pltpu.SemaphoreType.DMA,
            pltpu.SemaphoreType.DMA,
            pltpu.SemaphoreType.DMA((PREP_PIECES,)),
        ],
        compiler_params=pltpu.CompilerParams(vmem_limit_bytes=ALL_VMEM),
        cost_estimate=cost(300_000_000, 2_300_000),
        name="dispatch_rows",
    )(expert_ids.T, moe_input)
    arrived = lax.all_to_all(outgoing, ("grp", "dev"), split_axis=0, concat_axis=0, tiled=True)
    slot_shares = pl.pallas_call(
        slot_shares_kernel,
        out_shape=jax.ShapeDtypeStruct((2 * ROW_BLOCK, 2 * EXPERTS), jnp.bfloat16),
        in_specs=[whole(), whole()],
        out_specs=whole(),
        compiler_params=pltpu.CompilerParams(vmem_limit_bytes=16 << 20),
        cost_estimate=cost(1_000_000, 20_000),
        name="slot_shares",
    )(expert_ids, route_scores)
    return outgoing, arrived, slot_shares


def expert_answers(arrived, w_gate, w_up, w_down, outgoing):
    in_hbm = pl.BlockSpec(memory_space=pltpu.HBM)
    return pl.pallas_call(
        ffn_kernel,
        out_shape=jax.ShapeDtypeStruct((EXPERTS, CHUNK, LANES), jnp.bfloat16),
        in_specs=[whole()] + [in_hbm] * 4,
        out_specs=in_hbm,
        input_output_aliases={4: 0},
        scratch_shapes=[
            pltpu.VMEM((DMODEL, FF), jnp.bfloat16),
            pltpu.VMEM((DMODEL, FF), jnp.bfloat16),
            pltpu.VMEM((FF, DMODEL), jnp.bfloat16),
            pltpu.VMEM((GROUPS, EXPERTS, 16, LANES), jnp.bfloat16),
            pltpu.VMEM((2 * EXPERTS, DMODEL), jnp.bfloat16),
            pltpu.SemaphoreType.DMA((3, FFN_PIECES)),
            pltpu.SemaphoreType.DMA((GROUPS,)),
        ],
        compiler_params=pltpu.CompilerParams(vmem_limit_bytes=FFN_VMEM),
        cost_estimate=cost(4_800_000_000, 23_000_000),
        name="expert_ffn",
    )(arrived, w_gate, w_up, w_down, outgoing)


def collected(answers, slot_shares):
    returned = lax.all_to_all(answers, ("grp", "dev"), split_axis=0, concat_axis=0, tiled=True)
    return pl.pallas_call(
        combine_kernel,
        out_shape=jax.ShapeDtypeStruct((ROW_BLOCK, DMODEL), jnp.bfloat16),
        in_specs=[whole(), whole()],
        out_specs=whole(),
        scratch_shapes=[pltpu.VMEM((2 * LANES, EXPERTS * 16), jnp.bfloat16)],
        compiler_params=pltpu.CompilerParams(vmem_limit_bytes=16 << 20),
        cost_estimate=cost(540_000_000, 3_300_000),
        name="weighted_sum",
    )(slot_shares, returned)


def body(
    queries,
    cache_keys,
    cache_values,
    own_len,
    ext_keys,
    ext_values,
    ext_len,
    new_key,
    new_value,
    moe_input,
    expert_ids,
    route_scores,
    w_gate,
    w_up,
    w_down,
):
    slot_count = cache_keys.shape[1]
    positions = jnp.arange(slot_count + 1, dtype=jnp.int32)[None, :]
    own_live = (positions < own_len[:, None]) | (positions == slot_count)
    own_keys = jnp.concatenate([cache_keys, new_key[:, None, :]], axis=1)
    own_values = jnp.concatenate([cache_values, new_value[:, None, :]], axis=1)
    own_part = partial_softmax(queries, own_keys, own_values, own_live)
    far_queries = partner(queries, "dev", 0)
    helped = partial_softmax(far_queries, ext_keys, ext_values, positions[:, :slot_count] < ext_len[:, None])
    packed = packed_part(helped)
    outgoing, arrived, slot_shares = dispatched(moe_input, expert_ids, route_scores)
    packed, arrived = tied(packed, arrived, TIE_VMEM)
    far_part = partner(packed, "dev", 0)
    answers, far_part = tied(expert_answers(arrived, w_gate, w_up, w_down, outgoing), far_part, LATE_TIE_VMEM)
    moe_out = collected(answers, slot_shares)
    attention_out = merge_parts(own_part, unpacked_part(far_part))
    return (attention_out, moe_out)


def solution(mesh):
    placed = (
        P(("grp", "dev"), None),
        P(("grp", "dev"), None, None),
        P(("grp", "dev"), None, None),
        P(("grp", "dev")),
        P(("grp", "dev"), None, None),
        P(("grp", "dev"), None, None),
        P(("grp", "dev")),
        P(("grp", "dev"), None),
        P(("grp", "dev"), None),
        P(("grp", "dev"), None),
        P(("grp", "dev"), None),
        P(("grp", "dev"), None),
        P(("grp", "dev"), None, None),
        P(("grp", "dev"), None, None),
        P(("grp", "dev"), None, None),
    )
    return jax.shard_map(
        body,
        mesh=mesh,
        in_specs=placed,
        out_specs=(P(("grp", "dev"), None), P(("grp", "dev"), None)),
        check_vma=False,
    )
```

time: 106 us -> 94.4 us (0.89)
  local copies, waits for them, and re-layouts: 9.65 us -> 5.83 us
  waiting for transfers between devices: 46.2 us -> 42.9 us
  other arithmetic: 4.82 us -> 2.9 us
  Pallas kernels: 16.7 us -> 15.2 us
    ppermute x3 -> x2, waiting for transfers between devices: 9 us -> 0.01 us  [partner(): return lax.ppermute(block, axis, route)]
    all_to_all x2, waiting for transfers between devices: 37.2 us -> 42.9 us  [the longest x1 24.2 us: dispatched(): lax.all_to_all(outgoing, ('grp', 'dev'), split_axis=0, concat_axis=0, til...]
    unnamed x25 -> x19, local copies, waits for them, and re-layouts: 5.34 us -> 1.87 us
    convert_element_type x1, other arithmetic: 3.12 us -> 1.52 us  [merge_parts(): return merged.reshape(merged.shape[0], -1).astype(jnp.bfloat16)]
    pallas_call x4 -> x6, Pallas kernels: 16.7 us -> 15.2 us  [the longest x1 10.8 us: expert_answers(): pl.pallas_call(ffn_kernel, out_shape=jax.ShapeDtypeStruct((EXPERTS, CHUNK...]
    dot_general x2, matrix products: 4.45 us -> 3.38 us  [partial_softmax(): numerator = jnp.einsum('rkgs,rskh->rkgh', weights, value_flat)]
    ppermute x3 -> x2, starting transfers between devices: 2.84 us -> 2.19 us  [partner(): return lax.ppermute(block, axis, route)]
  transfers between devices with their start and end apart: 5 -> 4, of which waited for: 3 -> 2; matrix products, arithmetic and copies ran while one was open for 17% -> 16% of each run, Pallas kernels for 3% -> 15%
where the time goes in v2:
time: 94.4 us; the launch traced here: 93.8 us
  waiting for transfers between devices  42.9 us (45%)
  starting transfers between devices  19.5 us (21%)
  Pallas kernels  15.2 us (16%)
  matrix products  6.57 us (7%)
  local copies, waits for them, and re-layouts  5.83 us (6%)
  other arithmetic  2.9 us (3%)
    all_to_all x1, waiting for transfers between devices, dispatched(): lax.all_to_all(outgoing, ('grp', 'dev'), split_axis=0, concat_axis=0, til...  24.2 us
    all_to_all x1, waiting for transfers between devices, collected(): lax.all_to_all(answers, ('grp', 'dev'), split_axis=0, concat_axis=0, tile...  18.7 us
    all_to_all x1, starting transfers between devices, dispatched(): lax.all_to_all(outgoing, ('grp', 'dev'), split_axis=0, concat_axis=0, til...  10.8 us
    pallas_call x1, Pallas kernels, expert_answers(): pl.pallas_call(ffn_kernel, out_shape=jax.ShapeDtypeStruct((EXPERTS, CHUNK...  10.8 us
    all_to_all x1, starting transfers between devices, collected(): lax.all_to_all(answers, ('grp', 'dev'), split_axis=0, concat_axis=0, tile...  6.47 us
    dot_general x2, matrix products, partial_softmax(): numerator = jnp.einsum('rkgs,rskh->rkgh', weights, value_flat)  3.38 us
    dot_general x2, matrix products, partial_softmax(): jnp.einsum('rkgh,rskh->rkgs', query_flat, key_flat)  3.19 us
    pallas_call x1, Pallas kernels, dispatched(): pl.pallas_call(dispatch_kernel, out_shape=exchange, in_specs=[in_hbm, in_...  2.63 us
  transfers between devices with their start and end apart: 4, of which 2 were waited for; matrix products, arithmetic and copies ran while one was open for 16% of the time, Pallas kernels for 15%

profile of v2, /device:TPU:5, one launch (start us, length us, event | category | flops | bytes accessed | tf_op | source)
XLA Modules:
  0.0 93.8 jit_solution(12020496648339667515)
XLA Ops:
  0.6 0.0 copy-start
  0.6 1.4 %collective-permute-start = (bf16[16,8192]{1,0:T(8,128)(2,1)}, bf16[16,8192]{1,0:T(8,128)(2,1)S(1)}, u32[]{:S(2)}, u32[]{:S(2)}) collective-permute-start(bf16[16,8192]{1,0:T(8,128)(2,1)} %param.15), channel_id=1, source_target_pairs={{0,1},{1,0},{2,3},{3,2},{4,5},{5,4},{6,7},{7,6},{8,9},{9,8},{10,11... | collective-permute-start | bytes 786440 | tf_op jit(solution)/shard_map/ppermute | solution.py:35
  2.0 2.6 %dispatch_rows.1.old_hbm = bf16[128,64,128]{2,1,0:T(8,128)(2,1)} custom-call(s32[8,16]{1,0:T(8,128)} %bitcast.70, bf16[16,4096]{1,0:T(8,128)(2,1)} %x_hbm.1), custom_call_target="tpu_custom_call" | custom-call | flops 300000000 | bytes 2300000 | tf_op jit(solution)/shard_map/dispatch_rows/pallas_call | solution.py:342
  4.7 0.0 copy-start.5
  4.7 10.8 %all-to-all-start = ((bf16[128,64,128]{2,1,0:T(8,128)(2,1)}), bf16[128,64,128]{2,1,0:T(8,128)(2,1)S(1)}, u32[]{:S(2)}, u32[]{:S(2)}) async-start(bf16[128,64,128]{2,1,0:T(8,128)(2,1)} %dispatch_rows.1.old_hbm), calls=%async_computation | async-start | bytes 4194304 | tf_op jit(solution)/shard_map/all_to_all | solution.py:362
  15.5 0.0 copy-done.5
  15.5 0.1 broadcast_compare_fusion
  15.6 0.1 pad.5.clone
  15.7 0.0 copy-done
  15.7 0.9 copy_bitcast_fusion.1
  16.6 0.0 collective-permute-done
  16.7 1.5 %select_reduce_fusion = (f32[16,4,16]{2,1,0:T(4,128)S(1)}, f32[16,4,16,32]{3,2,1,0:T(8,128)S(1)}) fusion(pred[16,32]{1,0:T(8,128)(4,1)S(1)} %broadcast_compare_fusion, bf16[16,4,16,128]{3,2,1,0:T(8,128)(2,1)S(1)} %bitcast.62, bf16[16,32,512]{2,1,0:T(8,128)(2,1)} %param.19), kind=kOutput, calls=%fused_computation.23 | convolution fusion | flops 8485888 | bytes 922112 | tf_op jit(solution)/shard_map/rkgh,rskh->rkgs/dot_general | solution.py:44
  18.2 0.1 reduce_max.25
  18.3 0.4 fusion.17
  18.7 0.1 reshape.194
  18.8 0.1 maximum_maximum_fusion
  18.9 1.4 %fusion.7 = f32[16,4,16,128]{3,2,1,0:T(8,128)S(1)} fusion(f32[16,4,16,32]{3,2,1,0:T(8,128)S(1)} %get-tuple-element.23, f32[16,4,16]{2,1,0:T(4,128)S(1)} %is-finite_select_fusion, pred[16,32]{1,0:T(8,128)(4,1)S(1)} %broadcast_compare_fusion, bf16[16,32,512]{2,1,0:T(8,128)(2,1)} %param.20), kind=kOutput, calls=%fused_computation.9 | convolution fusion | flops 8454144 | bytes 1184256 | tf_op jit(solution)/shard_map/rkgs,rskh->rkgh/dot_general | solution.py:50
  20.3 0.2 fusion.12
  20.6 24.2 %all-to-all-done.two_ref = bf16[128,64,128]{2,1,0:T(8,128)(2,1)S(1)} async-done(((bf16[128,64,128]{2,1,0:T(8,128)(2,1)}), bf16[128,64,128]{2,1,0:T(8,128)(2,1)S(1)}, u32[]{:S(2)}, u32[]{:S(2)}) %all-to-all-start) | async-done | bytes 2097184 | tf_op jit(solution)/shard_map/all_to_all | solution.py:362
  44.8 0.8 collective-permute-start.1
  45.6 10.8 %expert_ffn.1.one_ref = bf16[128,64,128]{2,1,0:T(8,128)(2,1)} custom-call(bf16[128,64,128]{2,1,0:T(8,128)(2,1)S(1)} %get-tuple-element.6.x_ref, bf16[1,4096,768]{2,1,0:T(8,128)(2,1)} %gate_hbm.1, bf16[1,4096,768]{2,1,0:T(8,128)(2,1)} %up_hbm.1, bf16[1,768,4096]{2,1,0:T(8,128)(2,1)} %down_hbm.1, ...), custom_call_target="tpu_custom_call", output_to_operand_aliasing={{}: (4, {})} | custom-call | flops 4800000000 | bytes 23000000 | tf_op jit(solution)/shard_map/expert_ffn/pallas_call | solution.py:377
  56.4 0.0 collective-permute-done.1.two_ref
  56.4 0.0 copy-start.6
  56.4 0.0 copy-start.2
  56.4 0.0 copy-start.1
  56.4 0.0 copy-start.3
  56.4 6.5 %all-to-all-start.1 = ((bf16[128,64,128]{2,1,0:T(8,128)(2,1)}), bf16[128,64,128]{2,1,0:T(8,128)(2,1)S(1)}, u32[]{:S(2)}, u32[]{:S(2)}) async-start(bf16[128,64,128]{2,1,0:T(8,128)(2,1)} %get-tuple-element.9), calls=%async_computation.1 | async-start | bytes 4194304 | tf_op jit(solution)/shard_map/all_to_all | solution.py:399
  62.9 0.0 copy-done.6
  62.9 0.0 copy-start.4
  63.0 0.1 fusion.28
  63.0 0.0 copy-done.2
  63.0 0.1 copy.38.ids_ref
  63.1 0.0 copy-done.1
  63.1 0.8 copy.47
  63.9 0.0 copy-done.3
  63.9 1.7 %select_reduce_fusion.1 = (f32[16,4,16]{2,1,0:T(4,128)S(1)}, f32[16,4,33,16]{2,3,1,0:T(8,128)S(1)}) fusion(pred[16,33]{1,0:T(8,128)(4,1)S(1)} %fusion.28, bf16[16,4,16,128]{3,2,1,0:T(8,128)(2,1)} %bitcast.66, bf16[16,1,4,128]{3,1,2,0:T(2,128)(2,1)S(1)} %concatenate.32, bf16[16,32,4,128]{3,1,2,0:T(8,128)(2,1)} %copy_bitcast_fusion.1), kind=kOutput, calls=%fused_computation.25 | convolution fusion | flops 9832448 | bytes 942608 | tf_op jit(solution)/shard_map/rkgh,rskh->rkgs/dot_general | solution.py:44
  65.5 0.1 reduce_max.23
  65.6 0.4 fusion.16
  66.1 0.1 reshape.196
  66.2 1.4 %concatenate.33 = bf16[16,1,4,128]{3,1,2,0:T(2,128)(2,1)} reshape(bf16[16,512]{1,0:T(8,128)(2,1)} %param.23) | data formatting | bytes 32768 | tf_op jit(solution)/shard_map/concatenate | solution.py:433
  67.5 0.0 copy-done.4
  67.5 0.1 copy.39.scores_ref
  67.6 0.2 slot_shares.1.shares_ref
  67.8 1.1 %copy_bitcast_fusion = bf16[16,32,4,128]{3,1,2,0:T(8,128)(2,1)S(1)} fusion(bf16[16,32,512]{2,1,0:T(8,128)(2,1)} %param.17), kind=kLoop, calls=%fused_computation.14 | loop fusion | bytes 1048576 | tf_op jit(solution)/shard_map/concatenate | solution.py:433
  69.0 2.0 %fusion.3 = f32[16,4,16,128]{3,2,1,0:T(8,128)} fusion(bf16[16,1,4,128]{3,1,2,0:T(2,128)(2,1)} %concatenate.33, bf16[16,32,4,128]{3,1,2,0:T(8,128)(2,1)S(1)} %copy_bitcast_fusion, f32[16,4,33,16]{2,3,1,0:T(8,128)S(1)} %get-tuple-element.21, f32[16,4,16]{2,1,0:T(4,128)S(1)} %is-finite_select_fusion.1, pred[16,33]{1,0:T(8,128)(4,1)S(1)} %fusion.28), kind=kOutput, calls=%fused_computation.5 | convolution fusion | flops 9799680 | bytes 1204752 | tf_op jit(solution)/shard_map/rkgs,rskh->rkgh/dot_general | solution.py:50
  70.9 0.1 reshape.197
  71.1 1.5 %fusion.15 = bf16[16,64,128]{2,1,0:T(8,128)(2,1)S(1)} fusion(f32[16,4,16,128]{3,2,1,0:T(8,128)} %fusion.3, f32[16,64]{1,0:T(8,128)S(1)} %get-tuple-element.10, f32[16,64]{1,0:T(8,128)S(1)} %get-tuple-element.12, bf16[16,66,128]{2,1,0:T(8,128)(2,1)S(1)} %get-tuple-element.8, f32[16,64]{1,0:T(8,128)S(1)} %get-tuple-element.11), kind=kLoop, calls=%fused_computation.21 | loop fusion | flops 786432 | bytes 1060864 | tf_op jit(solution)/shard_map/convert_element_type | solution.py:103
  72.6 0.9 copy.63
  73.5 18.7 %all-to-all-done.1.back_ref = bf16[128,64,128]{2,1,0:T(8,128)(2,1)S(1)} async-done(((bf16[128,64,128]{2,1,0:T(8,128)(2,1)}), bf16[128,64,128]{2,1,0:T(8,128)(2,1)S(1)}, u32[]{:S(2)}, u32[]{:S(2)}) %all-to-all-start.1) | async-done | bytes 2097184 | tf_op jit(solution)/shard_map/all_to_all | solution.py:399
  92.2 1.6 %weighted_sum.1 = bf16[16,4096]{1,0:T(8,128)(2,1)} custom-call(bf16[32,256]{1,0:T(8,128)(2,1)S(1)} %slot_shares.1.shares_ref, bf16[128,64,128]{2,1,0:T(8,128)(2,1)S(1)} %all-to-all-done.1.back_ref), custom_call_target="tpu_custom_call" | custom-call | flops 540000000 | bytes 3300000 | tf_op jit(solution)/shard_map/weighted_sum/pallas_call | solution.py:400
  (16 shorter events, 0.2 us)
Async XLA Ops:
  0.6 15.1 %copy-start = (bf16[16,32,512]{2,1,0:T(8,128)(2,1)S(1)}, bf16[16,32,512]{2,1,0:T(8,128)(2,1)}, u32[]{:S(2)}) copy-start(bf16[16,32,512]{2,1,0:T(8,128)(2,1)} %param.16) | copy-start | bytes 1572868
  0.6 16.0 %collective-permute-start = (bf16[16,8192]{1,0:T(8,128)(2,1)}, bf16[16,8192]{1,0:T(8,128)(2,1)S(1)}, u32[]{:S(2)}, u32[]{:S(2)}) collective-permute-start(bf16[16,8192]{1,0:T(8,128)(2,1)} %param.15), channel_id=1, source_target_pairs={{0,1},{1,0},{2,3},{3,2},{4,5},{5,4},{6,7},{7,6},{8,9},{9,8},{10,11... | collective-permute-start | bytes 786440 | tf_op jit(solution)/shard_map/ppermute | solution.py:35
  4.7 10.8 %copy-start.5 = (s32[16]{0:T(128)S(1)}, s32[16]{0:T(128)}, u32[]{:S(2)}) copy-start(s32[16]{0:T(128)} %param.21) | copy-start | bytes 196
  4.7 40.1 %all-to-all-start = ((bf16[128,64,128]{2,1,0:T(8,128)(2,1)}), bf16[128,64,128]{2,1,0:T(8,128)(2,1)S(1)}, u32[]{:S(2)}, u32[]{:S(2)}) async-start(bf16[128,64,128]{2,1,0:T(8,128)(2,1)} %dispatch_rows.1.old_hbm), calls=%async_computation | async-start | bytes 4194304 | tf_op jit(solution)/shard_map/all_to_all | solution.py:362
  44.8 11.6 %collective-permute-start.1 = (bf16[16,66,128]{2,1,0:T(8,128)(2,1)S(1)}, bf16[16,66,128]{2,1,0:T(8,128)(2,1)S(1)}, u32[]{:S(2)}, u32[]{:S(2)}) collective-permute-start(bf16[16,66,128]{2,1,0:T(8,128)(2,1)S(1)} %get-tuple-element.7), channel_id=1, source_target_pairs={{0,1},{1,0},{2,3},{3,2},{4,5},{5,4},{6,7},{7,6},{8,9},{9,8},{10,11... | collective-permute-start | bytes 811016 | tf_op jit(solution)/shard_map/ppermute | solution.py:35
  56.4 6.5 %copy-start.6 = (s32[16]{0:T(128)S(1)}, s32[16]{0:T(128)}, u32[]{:S(2)}) copy-start(s32[16]{0:T(128)} %param.18) | copy-start | bytes 196
  56.4 6.6 %copy-start.2 = (s32[16,8]{0,1:T(8,128)S(1)}, s32[16,8]{0,1:T(8,128)}, u32[]{:S(2)}) copy-start(s32[16,8]{0,1:T(8,128)} %param.25) | copy-start | bytes 1540
  56.4 6.7 %copy-start.1 = (bf16[16,8192]{1,0:T(8,128)(2,1)S(1)}, bf16[16,8192]{1,0:T(8,128)(2,1)}, u32[]{:S(2)}) copy-start(bf16[16,8192]{1,0:T(8,128)(2,1)} %param.15) | copy-start | bytes 786436
  56.4 7.4 %copy-start.3 = (bf16[16,512]{1,0:T(8,128)(2,1)S(1)}, bf16[16,512]{1,0:T(8,128)(2,1)}, u32[]{:S(2)}) copy-start(bf16[16,512]{1,0:T(8,128)(2,1)} %param.22) | copy-start | bytes 49156
  56.4 35.8 %all-to-all-start.1 = ((bf16[128,64,128]{2,1,0:T(8,128)(2,1)}), bf16[128,64,128]{2,1,0:T(8,128)(2,1)S(1)}, u32[]{:S(2)}, u32[]{:S(2)}) async-start(bf16[128,64,128]{2,1,0:T(8,128)(2,1)} %get-tuple-element.9), calls=%async_computation.1 | async-start | bytes 4194304 | tf_op jit(solution)/shard_map/all_to_all | solution.py:399
  62.9 4.6 %copy-start.4 = (f32[16,8]{0,1:T(8,128)S(1)}, f32[16,8]{0,1:T(8,128)}, u32[]{:S(2)}) copy-start(f32[16,8]{0,1:T(8,128)} %param.26) | copy-start | bytes 1540

commit v3 on v2

--- a/solution.py
+++ b/solution.py
@@ -18,10 +18,9 @@
 CHUNK = 64
 PREP_PIECES = 8
 FFN_PIECES = 8
-FFN_AHEAD = 3
+FFN_AHEAD = 4
 ALL_VMEM = 60 << 20
 FFN_VMEM = 48 << 20
-TIE_VMEM = 16 << 20
 LATE_TIE_VMEM = 16 << 20
 
 
@@ -436,7 +435,6 @@
     helped = partial_softmax(far_queries, ext_keys, ext_values, positions[:, :slot_count] < ext_len[:, None])
     packed = packed_part(helped)
     outgoing, arrived, slot_shares = dispatched(moe_input, expert_ids, route_scores)
-    packed, arrived = tied(packed, arrived, TIE_VMEM)
     far_part = partner(packed, "dev", 0)
     answers, far_part = tied(expert_answers(arrived, w_gate, w_up, w_down, outgoing), far_part, LATE_TIE_VMEM)
     moe_out = collected(answers, slot_shares)

time: 94.4 us -> 92.6 us (0.981)
  waiting for transfers between devices: 42.9 us -> 41.6 us
    all_to_all x1, waiting for transfers between devices: 24.2 us -> 22.9 us  [dispatched(): lax.all_to_all(outgoing, ('grp', 'dev'), split_axis=0, concat_axis=0, til...]
  transfers between devices with their start and end apart: 4 -> 4, of which waited for: 2 -> 2; matrix products, arithmetic and copies ran while one was open for 16% -> 17% of each run, Pallas kernels for 15% -> 15%
where the time goes in v3:
time: 92.6 us; the launch traced here: 92 us
  waiting for transfers between devices  41.6 us (45%)
  starting transfers between devices  19.3 us (21%)
  Pallas kernels  14.9 us (16%)
  matrix products  6.55 us (7%)
  local copies, waits for them, and re-layouts  5.82 us (6%)
  other arithmetic  2.9 us (3%)
    all_to_all x1, waiting for transfers between devices, dispatched(): lax.all_to_all(outgoing, ('grp', 'dev'), split_axis=0, concat_axis=0, til...  22.9 us
    all_to_all x1, waiting for transfers between devices, collected(): lax.all_to_all(answers, ('grp', 'dev'), split_axis=0, concat_axis=0, tile...  18.7 us
    all_to_all x1, starting transfers between devices, dispatched(): lax.all_to_all(outgoing, ('grp', 'dev'), split_axis=0, concat_axis=0, til...  10.8 us
    pallas_call x1, Pallas kernels, expert_answers(): pl.pallas_call(ffn_kernel, out_shape=jax.ShapeDtypeStruct((EXPERTS, CHUNK...  10.5 us
    all_to_all x1, starting transfers between devices, collected(): lax.all_to_all(answers, ('grp', 'dev'), split_axis=0, concat_axis=0, tile...  5.88 us
    dot_general x2, matrix products, partial_softmax(): numerator = jnp.einsum('rkgs,rskh->rkgh', weights, value_flat)  3.37 us
    dot_general x2, matrix products, partial_softmax(): jnp.einsum('rkgh,rskh->rkgs', query_flat, key_flat)  3.18 us
    ppermute x2, starting transfers between devices, partner(): return lax.ppermute(block, axis, route)  2.64 us
  transfers between devices with their start and end apart: 4, of which 2 were waited for; matrix products, arithmetic and copies ran while one was open for 17% of the time, Pallas kernels for 15%

profile of v3, /device:TPU:5, one launch (start us, length us, event | category | flops | bytes accessed | tf_op | source)
XLA Modules:
  0.0 92.0 jit_solution(4504190185061994131)
XLA Ops:
  0.6 0.0 copy-start
  0.6 1.4 %collective-permute-start = (bf16[16,8192]{1,0:T(8,128)(2,1)}, bf16[16,8192]{1,0:T(8,128)(2,1)S(1)}, u32[]{:S(2)}, u32[]{:S(2)}) collective-permute-start(bf16[16,8192]{1,0:T(8,128)(2,1)} %param.15), channel_id=1, source_target_pairs={{0,1},{1,0},{2,3},{3,2},{4,5},{5,4},{6,7},{7,6},{8,9},{9,8},{10,11... | collective-permute-start | bytes 786440 | tf_op jit(solution)/shard_map/ppermute | solution.py:34
  2.0 2.6 %dispatch_rows.1.old_hbm = bf16[128,64,128]{2,1,0:T(8,128)(2,1)} custom-call(s32[8,16]{1,0:T(8,128)} %bitcast.70, bf16[16,4096]{1,0:T(8,128)(2,1)} %x_hbm.1), custom_call_target="tpu_custom_call" | custom-call | flops 300000000 | bytes 2300000 | tf_op jit(solution)/shard_map/dispatch_rows/pallas_call | solution.py:341
  4.7 0.0 copy-start.5
  4.7 10.8 %all-to-all-start = ((bf16[128,64,128]{2,1,0:T(8,128)(2,1)}), bf16[128,64,128]{2,1,0:T(8,128)(2,1)S(1)}, u32[]{:S(2)}, u32[]{:S(2)}) async-start(bf16[128,64,128]{2,1,0:T(8,128)(2,1)} %dispatch_rows.1.old_hbm), calls=%async_computation | async-start | bytes 4194304 | tf_op jit(solution)/shard_map/all_to_all | solution.py:361
  15.5 0.0 copy-done.5
  15.5 0.1 broadcast_compare_fusion
  15.6 0.1 pad.5.clone
  15.7 0.0 copy-done
  15.7 0.9 copy_bitcast_fusion.1
  16.6 0.0 collective-permute-done
  16.6 1.5 %select_reduce_fusion = (f32[16,4,16]{2,1,0:T(4,128)S(1)}, f32[16,4,16,32]{3,2,1,0:T(8,128)S(1)}) fusion(pred[16,32]{1,0:T(8,128)(4,1)S(1)} %broadcast_compare_fusion, bf16[16,4,16,128]{3,2,1,0:T(8,128)(2,1)S(1)} %bitcast.62, bf16[16,32,512]{2,1,0:T(8,128)(2,1)} %param.19), kind=kOutput, calls=%fused_computation.23 | convolution fusion | flops 8485888 | bytes 922112 | tf_op jit(solution)/shard_map/rkgh,rskh->rkgs/dot_general | solution.py:43
  18.2 0.1 reduce_max.25
  18.3 0.4 fusion.17
  18.7 0.1 reshape.194
  18.8 0.1 maximum_maximum_fusion
  18.9 1.4 %fusion.7 = f32[16,4,16,128]{3,2,1,0:T(8,128)S(1)} fusion(f32[16,4,16,32]{3,2,1,0:T(8,128)S(1)} %get-tuple-element.19, f32[16,4,16]{2,1,0:T(4,128)S(1)} %is-finite_select_fusion, pred[16,32]{1,0:T(8,128)(4,1)S(1)} %broadcast_compare_fusion, bf16[16,32,512]{2,1,0:T(8,128)(2,1)} %param.20), kind=kOutput, calls=%fused_computation.9 | convolution fusion | flops 8454144 | bytes 1184256 | tf_op jit(solution)/shard_map/rkgs,rskh->rkgh/dot_general | solution.py:49
  20.3 0.2 fusion.12
  20.6 1.3 %collective-permute-start.1 = (bf16[16,66,128]{2,1,0:T(8,128)(2,1)S(1)}, bf16[16,66,128]{2,1,0:T(8,128)(2,1)S(1)}, u32[]{:S(2)}, u32[]{:S(2)}) collective-permute-start(bf16[16,66,128]{2,1,0:T(8,128)(2,1)S(1)} %pad_maximum_fusion), channel_id=1, source_target_pairs={{0,1},{1,0},{2,3},{3,2},{4,5},{5,4},{6,7},{7,6},{8,9},{9,8},{10,11... | collective-permute-start | bytes 811016 | tf_op jit(solution)/shard_map/ppermute | solution.py:34
  21.8 22.9 %all-to-all-done.x_ref = bf16[128,64,128]{2,1,0:T(8,128)(2,1)S(1)} async-done(((bf16[128,64,128]{2,1,0:T(8,128)(2,1)}), bf16[128,64,128]{2,1,0:T(8,128)(2,1)S(1)}, u32[]{:S(2)}, u32[]{:S(2)}) %all-to-all-start) | async-done | bytes 2097184 | tf_op jit(solution)/shard_map/all_to_all | solution.py:361
  44.7 10.5 %expert_ffn.1.one_ref = bf16[128,64,128]{2,1,0:T(8,128)(2,1)} custom-call(bf16[128,64,128]{2,1,0:T(8,128)(2,1)S(1)} %all-to-all-done.x_ref, bf16[1,4096,768]{2,1,0:T(8,128)(2,1)} %gate_hbm.1, bf16[1,4096,768]{2,1,0:T(8,128)(2,1)} %up_hbm.1, bf16[1,768,4096]{2,1,0:T(8,128)(2,1)} %down_hbm.1, ...), custom_call_target="tpu_custom_call", output_to_operand_aliasing={{}: (4, {})} | custom-call | flops 4800000000 | bytes 23000000 | tf_op jit(solution)/shard_map/expert_ffn/pallas_call | solution.py:376
  55.2 0.0 collective-permute-done.1.two_ref
  55.3 0.0 copy-start.6
  55.3 0.0 copy-start.2
  55.3 0.0 copy-start.1
  55.3 0.0 copy-start.3
  55.3 5.9 %all-to-all-start.1 = ((bf16[128,64,128]{2,1,0:T(8,128)(2,1)}), bf16[128,64,128]{2,1,0:T(8,128)(2,1)S(1)}, u32[]{:S(2)}, u32[]{:S(2)}) async-start(bf16[128,64,128]{2,1,0:T(8,128)(2,1)} %get-tuple-element.5), calls=%async_computation.1 | async-start | bytes 4194304 | tf_op jit(solution)/shard_map/all_to_all | solution.py:398
  61.2 0.0 copy-done.6
  61.2 0.0 copy-start.4
  61.2 0.1 fusion.28
  61.3 0.0 copy-done.2
  61.3 0.1 copy.36.ids_ref
  61.4 0.0 copy-done.1
  61.4 0.8 copy.45
  62.1 0.0 copy-done.3
  62.1 1.7 %select_reduce_fusion.1 = (f32[16,4,16]{2,1,0:T(4,128)S(1)}, f32[16,4,33,16]{2,3,1,0:T(8,128)S(1)}) fusion(pred[16,33]{1,0:T(8,128)(4,1)S(1)} %fusion.28, bf16[16,4,16,128]{3,2,1,0:T(8,128)(2,1)} %bitcast.66, bf16[16,1,4,128]{3,1,2,0:T(2,128)(2,1)S(1)} %concatenate.32, bf16[16,32,4,128]{3,1,2,0:T(8,128)(2,1)} %copy_bitcast_fusion.1), kind=kOutput, calls=%fused_computation.25 | convolution fusion | flops 9832448 | bytes 942608 | tf_op jit(solution)/shard_map/rkgh,rskh->rkgs/dot_general | solution.py:43
  63.8 0.1 reduce_max.23
  63.9 0.4 fusion.16
  64.3 0.1 reshape.196
  64.4 1.4 %concatenate.33 = bf16[16,1,4,128]{3,1,2,0:T(2,128)(2,1)} reshape(bf16[16,512]{1,0:T(8,128)(2,1)} %param.23) | data formatting | bytes 32768 | tf_op jit(solution)/shard_map/concatenate | solution.py:432
  65.8 0.0 copy-done.4
  65.8 0.1 copy.37.scores_ref
  65.8 0.2 slot_shares.1.shares_ref
  66.1 1.1 %copy_bitcast_fusion = bf16[16,32,4,128]{3,1,2,0:T(8,128)(2,1)S(1)} fusion(bf16[16,32,512]{2,1,0:T(8,128)(2,1)} %param.17), kind=kLoop, calls=%fused_computation.14 | loop fusion | bytes 1048576 | tf_op jit(solution)/shard_map/concatenate | solution.py:432
  67.2 2.0 %fusion.3 = f32[16,4,16,128]{3,2,1,0:T(8,128)} fusion(bf16[16,1,4,128]{3,1,2,0:T(2,128)(2,1)} %concatenate.33, bf16[16,32,4,128]{3,1,2,0:T(8,128)(2,1)S(1)} %copy_bitcast_fusion, f32[16,4,33,16]{2,3,1,0:T(8,128)S(1)} %get-tuple-element.17, f32[16,4,16]{2,1,0:T(4,128)S(1)} %is-finite_select_fusion.1, pred[16,33]{1,0:T(8,128)(4,1)S(1)} %fusion.28), kind=kOutput, calls=%fused_computation.5 | convolution fusion | flops 9799680 | bytes 1204752 | tf_op jit(solution)/shard_map/rkgs,rskh->rkgh/dot_general | solution.py:49
  69.2 0.1 reshape.197
  69.3 1.5 %fusion.15 = bf16[16,64,128]{2,1,0:T(8,128)(2,1)S(1)} fusion(f32[16,4,16,128]{3,2,1,0:T(8,128)} %fusion.3, f32[16,64]{1,0:T(8,128)S(1)} %get-tuple-element.6, f32[16,64]{1,0:T(8,128)S(1)} %get-tuple-element.8, bf16[16,66,128]{2,1,0:T(8,128)(2,1)S(1)} %get-tuple-element.4, f32[16,64]{1,0:T(8,128)S(1)} %get-tuple-element.7), kind=kLoop, calls=%fused_computation.21 | loop fusion | flops 786432 | bytes 1060864 | tf_op jit(solution)/shard_map/convert_element_type | solution.py:102
  70.9 0.9 copy.61
  71.7 18.7 %all-to-all-done.1.back_ref = bf16[128,64,128]{2,1,0:T(8,128)(2,1)S(1)} async-done(((bf16[128,64,128]{2,1,0:T(8,128)(2,1)}), bf16[128,64,128]{2,1,0:T(8,128)(2,1)S(1)}, u32[]{:S(2)}, u32[]{:S(2)}) %all-to-all-start.1) | async-done | bytes 2097184 | tf_op jit(solution)/shard_map/all_to_all | solution.py:398
  90.5 1.6 %weighted_sum.1 = bf16[16,4096]{1,0:T(8,128)(2,1)} custom-call(bf16[32,256]{1,0:T(8,128)(2,1)S(1)} %slot_shares.1.shares_ref, bf16[128,64,128]{2,1,0:T(8,128)(2,1)S(1)} %all-to-all-done.1.back_ref), custom_call_target="tpu_custom_call" | custom-call | flops 540000000 | bytes 3300000 | tf_op jit(solution)/shard_map/weighted_sum/pallas_call | solution.py:399
  (15 shorter events, 0.2 us)
Async XLA Ops:
  0.6 15.1 %copy-start = (bf16[16,32,512]{2,1,0:T(8,128)(2,1)S(1)}, bf16[16,32,512]{2,1,0:T(8,128)(2,1)}, u32[]{:S(2)}) copy-start(bf16[16,32,512]{2,1,0:T(8,128)(2,1)} %param.16) | copy-start | bytes 1572868
  0.6 15.9 %collective-permute-start = (bf16[16,8192]{1,0:T(8,128)(2,1)}, bf16[16,8192]{1,0:T(8,128)(2,1)S(1)}, u32[]{:S(2)}, u32[]{:S(2)}) collective-permute-start(bf16[16,8192]{1,0:T(8,128)(2,1)} %param.15), channel_id=1, source_target_pairs={{0,1},{1,0},{2,3},{3,2},{4,5},{5,4},{6,7},{7,6},{8,9},{9,8},{10,11... | collective-permute-start | bytes 786440 | tf_op jit(solution)/shard_map/ppermute | solution.py:34
  4.7 10.8 %copy-start.5 = (s32[16]{0:T(128)S(1)}, s32[16]{0:T(128)}, u32[]{:S(2)}) copy-start(s32[16]{0:T(128)} %param.21) | copy-start | bytes 196
  4.7 40.0 %all-to-all-start = ((bf16[128,64,128]{2,1,0:T(8,128)(2,1)}), bf16[128,64,128]{2,1,0:T(8,128)(2,1)S(1)}, u32[]{:S(2)}, u32[]{:S(2)}) async-start(bf16[128,64,128]{2,1,0:T(8,128)(2,1)} %dispatch_rows.1.old_hbm), calls=%async_computation | async-start | bytes 4194304 | tf_op jit(solution)/shard_map/all_to_all | solution.py:361
  20.6 34.7 %collective-permute-start.1 = (bf16[16,66,128]{2,1,0:T(8,128)(2,1)S(1)}, bf16[16,66,128]{2,1,0:T(8,128)(2,1)S(1)}, u32[]{:S(2)}, u32[]{:S(2)}) collective-permute-start(bf16[16,66,128]{2,1,0:T(8,128)(2,1)S(1)} %pad_maximum_fusion), channel_id=1, source_target_pairs={{0,1},{1,0},{2,3},{3,2},{4,5},{5,4},{6,7},{7,6},{8,9},{9,8},{10,11... | collective-permute-start | bytes 811016 | tf_op jit(solution)/shard_map/ppermute | solution.py:34
  55.3 5.9 %copy-start.6 = (s32[16]{0:T(128)S(1)}, s32[16]{0:T(128)}, u32[]{:S(2)}) copy-start(s32[16]{0:T(128)} %param.18) | copy-start | bytes 196
  55.3 6.0 %copy-start.2 = (s32[16,8]{0,1:T(8,128)S(1)}, s32[16,8]{0,1:T(8,128)}, u32[]{:S(2)}) copy-start(s32[16,8]{0,1:T(8,128)} %param.25) | copy-start | bytes 1540
  55.3 6.1 %copy-start.1 = (bf16[16,8192]{1,0:T(8,128)(2,1)S(1)}, bf16[16,8192]{1,0:T(8,128)(2,1)}, u32[]{:S(2)}) copy-start(bf16[16,8192]{1,0:T(8,128)(2,1)} %param.15) | copy-start | bytes 786436
  55.3 6.8 %copy-start.3 = (bf16[16,512]{1,0:T(8,128)(2,1)S(1)}, bf16[16,512]{1,0:T(8,128)(2,1)}, u32[]{:S(2)}) copy-start(bf16[16,512]{1,0:T(8,128)(2,1)} %param.22) | copy-start | bytes 49156
  55.3 35.2 %all-to-all-start.1 = ((bf16[128,64,128]{2,1,0:T(8,128)(2,1)}), bf16[128,64,128]{2,1,0:T(8,128)(2,1)S(1)}, u32[]{:S(2)}, u32[]{:S(2)}) async-start(bf16[128,64,128]{2,1,0:T(8,128)(2,1)} %get-tuple-element.5), calls=%async_computation.1 | async-start | bytes 4194304 | tf_op jit(solution)/shard_map/all_to_all | solution.py:398
  61.2 4.6 %copy-start.4 = (f32[16,8]{0,1:T(8,128)S(1)}, f32[16,8]{0,1:T(8,128)}, u32[]{:S(2)}) copy-start(f32[16,8]{0,1:T(8,128)} %param.26) | copy-start | bytes 1540
